TPU v7x, 32 devices: a whole 2x2x4 slice. The times are simulated.
32 devices in a mesh: prot: 2 (over core), res: 4 (over z), mp: 4 (over y, x).
Axes of the slice: x: 2, y: 2, z: 4, core: 2. Of those that a mesh axis runs over, the one named last changes fastest.
Arguments:
- node_states: bfloat16 [8, 1024, 512], P('prot', 'res'), may hold values from -6 to 6
- edge_states: bfloat16 [8, 1024, 60, 192], P('prot', 'res', 'mp'), may hold values from -6 to 6
- neighbour_slots: int32 [8, 1024, 60], P('prot', 'res'), may hold values from 0 to 319, as said below
- send_rows: int32 [8, 4, 4, 16], P('prot', 'res'), may hold values from 0 to 255, as said below
- live_counts: int32 [8, 1024], P('prot', 'res'), may hold values from 0 to 60
- message_nodes: bfloat16 [2, 512, 512], P(None, None, 'mp'), may hold values from -0.15625 to 0.15625
- message_edges: bfloat16 [192, 512], replicated, may hold values from -0.15625 to 0.15625
- message_bias: bfloat16 [512], P('mp'), may hold values from -3 to 3
- message_output: bfloat16 [512, 512], P('mp'), may hold values from -0.75 to 0.75
- feedforward_weight: bfloat16 [512, 2048], P(None, 'mp'), may hold values from -0.25 to 0.25
- feedforward_bias: bfloat16 [2048], P('mp'), may hold values from -3 to 3
- feedforward_output: bfloat16 [2048, 512], P('mp'), may hold values from -0.1875 to 0.1875
- output_biases: bfloat16 [2, 512], replicated, may hold values from -2 to 2
- norm_gains: bfloat16 [2, 512], replicated, may hold values from 0.5 to 1.5
- norm_shifts: bfloat16 [2, 512], replicated, may hold values from -2 to 2
- update_weight: bfloat16 [1216, 192], replicated, may hold values from -0.15625 to 0.15625
- update_bias: bfloat16 [192], replicated, may hold values from -3 to 3
- update_output: bfloat16 [192, 192], replicated, may hold values from -0.625 to 0.625
- branch_bias: bfloat16 [192], replicated, may hold values from -2 to 2
- edge_gain: bfloat16 [192], replicated, may hold values from 0.5 to 1.5
- edge_shift: bfloat16 [192], replicated, may hold values from -2 to 2
- node_cotangent: bfloat16 [8, 1024, 512], P('prot', 'res'), may hold values from -6 to 6
- edge_cotangent: bfloat16 [8, 1024, 60, 192], P('prot', 'res', 'mp'), may hold values from -6 to 6
Outputs:
- node_result: bfloat16 [8, 1024, 512], P('prot', 'res')
- edge_result: bfloat16 [8, 1024, 60, 192], P('prot', 'res', 'mp')
- node_grad: bfloat16 [8, 1024, 512], P('prot', 'res')
- edge_grad: bfloat16 [8, 1024, 60, 192], P('prot', 'res', 'mp')
- message_nodes_grad: float32 [2, 512, 512], P(None, None, 'mp')
- message_edges_grad: float32 [192, 512], replicated
- message_bias_grad: float32 [512], P('mp')
- message_output_grad: float32 [512, 512], P('mp')
- feedforward_weight_grad: float32 [512, 2048], P(None, 'mp')
- feedforward_bias_grad: float32 [2048], P('mp')
- feedforward_output_grad: float32 [2048, 512], P('mp')
- output_biases_grad: float32 [2, 512], replicated
- norm_gains_grad: float32 [2, 512], replicated
- norm_shifts_grad: float32 [2, 512], replicated
- update_weight_grad: float32 [1216, 192], replicated
- update_bias_grad: float32 [192], replicated
- update_output_grad: float32 [192, 192], replicated
- branch_bias_grad: float32 [192], replicated
- edge_gain_grad: float32 [192], replicated
- edge_shift_grad: float32 [192], replicated
Inputs may be any that keep to these rules, and one draw needn't show every extreme that they name: send_rows[b,p,d,c] is a row of block p; for each pair of blocks the first entries (none when p = d, all 16 for at least one sender to each block) are distinct rows that block d may name, and the remaining entries are 0 and named by no slot. `neighbour_slots`: A slot below 256 names a row of the residue's own block; a larger slot s names entry (s - 256) % 16 of what block (s - 256) // 16 sends to the residue's block, and only entries that the promise on send_rows calls used; every used entry is named by some residue of the receiving block; the 60 slots of a residue are distinct.
All inputs are finite; a program needn't handle non-finite values.
Results may differ from a plain program's by a relative error of at most 0.025.
Values may be sent and summed in bfloat16 or wider, within the bound.
No kernel may reach another device: no remote copies, remote signals or barrier semaphores. Data moves between devices by JAX's collectives and lax.ppermute only.
A program may use at most 320 MiB of HBM per device.

v0:
```python
import functools

import jax
import jax.numpy as jnp
from jax import lax
from jax.experimental import pallas as pl
from jax.experimental.pallas import tpu as pltpu
from jax.sharding import PartitionSpec as P

EPSILON = 1e-05
F32 = jnp.float32
PINNED = ("prepare",)
BF16 = jnp.bfloat16
DEAD = -30000.0
CUBIC = 0.044715
ROOT = 0.7978845608028654


def dot(left, right):
    return jnp.dot(left, right, preferred_element_type=F32)


def dot_nt(left, right):
    return lax.dot_general(left, right, (((1,), (1,)), ((), ())), preferred_element_type=F32)


def gelu_pair(value):
    square = value * value
    gate = 0.5 + 0.5 * jnp.tanh(value * (ROOT + (ROOT * CUBIC) * square))
    out = value * gate
    slope = gate + (out - out * gate) * (2.0 * ROOT + (6.0 * ROOT * CUBIC) * square)
    return out, slope


def low(value):
    return jnp.asarray(value, BF16)


def gelu_pair_low(value):
    value = value.astype(BF16)
    square = value * value
    inner = value * (low(-2.0 * ROOT) + low(-2.0 * ROOT * CUBIC) * square)
    power = jnp.exp(jnp.minimum(inner, low(80.0)))
    gate = pl.reciprocal(low(1.0) + power, approx=True)
    out = value * gate
    slope = gate + (out * (power * gate)) * (low(2.0 * ROOT) + low(6.0 * ROOT * CUBIC) * square)
    return out, slope


def activation(value):
    return jax.nn.gelu(value, approximate=True)


def activation_grad(value, upstream):
    return jax.vjp(activation, value)[1](upstream)[0]


def norm_forward(value, gain, shift):
    centred = value - jnp.mean(value, axis=-1, keepdims=True)
    inverse = lax.rsqrt(jnp.mean(centred * centred, axis=-1, keepdims=True) + EPSILON)
    normed = centred * inverse
    return (normed * gain + shift, normed, inverse)


def norm_backward(upstream, normed, inverse, gain):
    scaled = upstream * gain
    inner = (
        scaled
        - jnp.mean(scaled, axis=-1, keepdims=True)
        - normed * jnp.mean(scaled * normed, axis=-1, keepdims=True)
    )
    return inverse * inner


def selector(slot_row, rows):
    positions = lax.broadcasted_iota(jnp.int16, (rows, slot_row.shape[1]), 0)
    return jnp.where(positions == slot_row.astype(jnp.int16), low(1.0), low(0.0))


def dot_tn(left, right):
    return lax.dot_general(left, right, (((0,), (0,)), ((), ())), preferred_element_type=F32)


def masked_table(fixed, term, dead):
    positions = lax.broadcasted_iota(jnp.int32, term.shape, 1)
    term = jnp.where(positions == dead, DEAD, term).astype(BF16)
    return jnp.concatenate([fixed, term], axis=1)


def message_forward_body(perm_ref, *refs, count, calls):
    edge_ref, slot_ref, node_ref, arrive_ref, fixed_ref, scale_ref = refs[:6]
    weights = refs[6 : 6 + count]
    others = refs[6 + count : 6 + 2 * count]
    refs = refs[6 + 2 * count :]
    slope_ref, mean_ref = refs[:2]
    parts = refs[2 : 2 + calls]
    weight_ref, table_ref, self_ref, sum_ref, operand_ref, value_ref = refs[2 + calls :]
    number = pl.program_id(0)
    group = operand_ref.shape[0]
    dead = perm_ref[count]
    steps, channels, lanes = edge_ref.shape[1:]
    width = node_ref.shape[2]

    @pl.when(number == 0)
    def _():
        fill_weights(perm_ref, weights, others, weight_ref, count)

    nodes = node_ref[0]
    arrive = arrive_ref[...].reshape(-1, width)
    pool = lanes + arrive.shape[0]
    rows = jnp.concatenate([nodes, arrive], axis=0)
    term = dot_nt(weight_ref[:, width : 2 * width], rows)
    table_ref[...] = masked_table(fixed_ref[...], term, dead)
    bias = weight_ref[:, 3 * width : 3 * width + 1].astype(F32)
    self_ref[...] = dot_nt(weight_ref[:, 0:width], nodes) + bias
    sum_ref[...] = jnp.zeros_like(sum_ref)

    def some(index, carry):
        spots = [index * group + spot for spot in range(group)]
        for spot in range(group):
            operand_ref[spot, 0:channels] = edge_ref[0, spots[spot]]
            operand_ref[spot, channels:] = selector(slot_ref[0, pl.ds(spots[spot], 1), :], pool)
        for spot in range(group):
            value_ref[spot] = dot(table_ref[...], operand_ref[spot])
        total = sum_ref[...]
        for spot in range(group):
            out, slope = gelu_pair_low(value_ref[spot] + self_ref[...])
            slope_ref[0, spots[spot]] = slope
            total = total + out.astype(F32)
        sum_ref[...] = total
        return carry

    lax.fori_loop(0, steps // group, some, 0)
    mean = (sum_ref[...] * scale_ref[0]).astype(BF16)
    mean_ref[0] = mean
    total = dot_tn(mean, weight_ref[:, 2 * width : 3 * width]).astype(BF16)
    for spot in range(calls):

        @pl.when(number == spot)
        def _(spot=spot):
            parts[spot][...] = total


def pack_body(perm_ref, nodes_ref, output_ref, bias_ref, send_ref, node_ref, pack_ref, leave_ref, all_ref, *, count):
    width = output_ref.shape[1]
    part = output_ref.shape[0]
    all_ref[:, 0:width] = nodes_ref[0].T
    all_ref[:, width : 2 * width] = nodes_ref[1].T
    all_ref[:, 2 * width : 3 * width] = output_ref[...]
    tall = lambda row: jnp.broadcast_to(row, (8, row.shape[1])).T[:, 0:1]
    bias = tall(bias_ref[...].astype(F32).reshape(1, -1)).astype(BF16)
    all_ref[:, 3 * width :] = jnp.broadcast_to(bias, (part, all_ref.shape[1] - 3 * width))
    half = part // 2
    start = pl.multiple_of(perm_ref[count + 1] * half, half)
    pack_ref[...] = all_ref[pl.ds(start, half), :]
    proteins, lanes, _ = node_ref.shape
    for spot in range(proteins):
        rows = tall(send_ref[spot : spot + 1, :].astype(F32))
        lane = lax.broadcasted_iota(jnp.int32, (rows.shape[0], lanes), 1).astype(F32)
        table = jnp.where(lane == rows, 1.0, 0.0).astype(BF16)
        leave_ref[:, spot] = dot(table, node_ref[spot]).astype(BF16).reshape(leave_ref[:, spot].shape)


def prepare_body(
    perm_ref,
    edge_ref,
    turned_ref,
    out_ref,
    hidden_bias_ref,
    gain_ref,
    shift_ref,
    branch_ref,
    wide_ref,
    biases_ref,
    gains_ref,
    shifts_ref,
    counts_ref,
    send_ref,
    node_ref,
    up_ref,
    wide_in_ref,
    wide_out_ref,
    weight_ref,
    weight_t_ref,
    column_ref,
    out_t_ref,
    turned_edge_ref,
    vector_ref,
    share_ref,
    table_ref,
    wide_bias_ref,
    own_node_ref,
    own_up_ref,
    block_ref,
    *,
    count,
):
    row = lambda ref: ref[...].astype(F32).reshape(1, -1)
    core = perm_ref[count + 1]
    half = wide_out_ref.shape[0] // 2
    start = pl.multiple_of(core * half, half)
    block_ref[0:half, :] = wide_in_ref[:, pl.ds(start, half)].T
    block_ref[half : 2 * half, :] = wide_out_ref[pl.ds(start, half), :]
    wide = row(wide_ref)
    line = jnp.where(core == 0, wide[:, 0:half], wide[:, half:])
    block_ref[2 * half :, 0:half] = jnp.broadcast_to(line, (16, half)).astype(BF16)
    block_ref[2 * half :, half:] = jnp.zeros((16, block_ref.shape[1] - half), BF16)
    part = edge_ref.shape[1] // count
    for spot in range(count):
        span = slice(spot * part, (spot + 1) * part)
        block = edge_ref[:, pl.ds(pl.multiple_of(perm_ref[spot] * part, part), part)]
        weight_ref[:, span] = block
        weight_t_ref[span, :] = block.T
    tall = lambda row: jnp.broadcast_to(row, (8, row.shape[1])).T[:, 0:1]
    channels = edge_ref.shape[0]
    lane = lax.broadcasted_iota(jnp.int32, (channels, 128), 1)
    column_ref[...] = jnp.where(
        lane == 0,
        tall(row(hidden_bias_ref)),
        jnp.where(lane == 1, tall(row(gain_ref)), tall(row(shift_ref))),
    )
    hidden = out_ref.shape[0]
    extra = out_t_ref.shape[1] - hidden
    lane = lax.broadcasted_iota(jnp.int32, (channels, extra), 1)
    last = jnp.where(lane == 0, tall(row(branch_ref)), 0.0).astype(BF16)
    out_t_ref[...] = jnp.concatenate([out_ref[...].T, last], axis=1)
    turned_edge_ref[...] = turned_ref[:, turned_ref.shape[1] - channels :].T
    vector_ref[0:2, :] = biases_ref[...].astype(F32)
    vector_ref[2:4, :] = gains_ref[...].astype(F32)
    vector_ref[4:6, :] = shifts_ref[...].astype(F32)
    vector_ref[6:8, :] = jnp.zeros((2, vector_ref.shape[1]), F32)
    me = perm_ref[0]
    pick = lambda value: jnp.sum(
        jnp.where(lax.broadcasted_iota(jnp.int32, value.shape, 0) == me, value, 0.0), axis=0, keepdims=True
    )
    counts = pick(counts_ref[...].astype(F32))
    share = counts * (1.0 / jnp.maximum(counts, 1.0))
    share_ref[...] = jnp.broadcast_to(tall(share), share_ref.shape)
    rows = tall(pick(send_ref[...].astype(F32)))
    lane = lax.broadcasted_iota(jnp.int32, table_ref.shape, 1).astype(F32)
    table_ref[...] = jnp.where(lane == rows, 1.0, 0.0).astype(BF16)
    wide_bias_ref[...] = jnp.broadcast_to(wide, wide_bias_ref.shape).astype(BF16)
    own_node_ref[...] = node_ref[...]
    own_up_ref[...] = up_ref[...]


def fill_weights(perm_ref, mine, other, target, count):
    core = perm_ref[count + 1]
    half = mine[0].shape[0]
    for spot in range(count):
        for place, value in ((core, mine[spot][...]), (1 - core, other[spot][...])):
            start = pl.multiple_of((2 * spot + place) * half, half)
            target[pl.ds(start, half), :] = value


def forward_body(*refs, count):
    parts = refs[:count]
    node_ref, share_ref, vector_ref, send_ref, turned_ref = refs[count : count + 5]
    blocks = list(refs[count + 5 : 2 * count + 5])
    blocks = blocks + [refs[2 * count + 5].at[spot] for spot in range(count)]
    one_ref, two_ref, first_ref, second_ref, leave_ref, term_ref, slope_ref = refs[2 * count + 6 :]
    total = parts[0][...].astype(F32)
    for spot in range(1, count):
        total = total + parts[spot][...].astype(F32)
    value = node_ref[0].astype(F32) + total + share_ref[:, 0:1] * vector_ref[0:1, :]
    one_ref[...] = value
    first_norm, _, _ = norm_forward(value, vector_ref[2:3, :], vector_ref[4:5, :])
    first_low = first_norm.astype(BF16)
    first_ref[...] = first_low
    value = first_norm + vector_ref[1:2, :]
    for spot in range(2 * count):
        block = blocks[spot]
        half = (block.shape[0] - 16) // 2
        pre = dot_nt(first_low, block[0:half, :]) + block[2 * half : 2 * half + 1, 0:half].astype(F32)
        out, slope = gelu_pair(pre)
        slope_ref[:, spot * half : (spot + 1) * half] = slope.astype(BF16)
        value = value + dot(out.astype(BF16), block[half : 2 * half, :])
    two_ref[...] = value
    second_norm, _, _ = norm_forward(value, vector_ref[3:4, :], vector_ref[5:6, :])
    second = second_norm.astype(BF16)
    second_ref[...] = second
    leave_ref[...] = dot(send_ref[...], second).astype(BF16)
    lanes, width = second.shape
    term_ref[:, 0:lanes] = dot_nt(turned_ref[:, 0:width], second).astype(BF16)
    term_ref[:, lanes:] = dot_nt(turned_ref[:, width : 2 * width], second).astype(BF16)


def update_body(perm_ref, *refs, count, calls, first_call, joint):
    edge_ref, slot_ref, up_ref = refs[:3]
    terms = refs[3 : 3 + calls]
    if joint:
        refs = refs[: 3 + calls] + refs[3:]
        hidden = refs[3 + 2 * calls].shape[0]
        remotes = [ref.at[hidden:, :] for ref in terms]
        terms = [ref.at[0:hidden, :] for ref in terms]
    else:
        remotes = refs[3 + calls : 3 + 2 * calls]
    turned_ref, column_ref, out_t_ref, out_ref, weight_ref = refs[3 + 2 * calls : 8 + 2 * calls]
    refs = refs[8 + 2 * calls :]
    if not first_call:
        start_ref = refs[0]
        refs = refs[2:]
    result_ref, part_ref = refs[:2]
    sums = refs[2 : 2 + calls]
    total_ref = refs[2 + calls]
    table_ref, self_ref, table_grad_ref, self_grad_ref = refs[3 + calls : 7 + calls]
    gain_grad_ref, shift_grad_ref, edge_grad_ref, out_grad_ref = refs[7 + calls : 11 + calls]
    gain_ref, shift_ref, operand_ref, out_low_ref, mixed_ref, grad_ref, product_ref, value_ref, slope_ref = refs[
        11 + calls :
    ]
    group = operand_ref.shape[1] // edge_ref.shape[3]
    number = pl.program_id(0)
    dead = perm_ref[count]
    steps, channels, lanes = edge_ref.shape[1:]
    hidden = turned_ref.shape[0]
    width = remotes[0].shape[1]
    pool = lanes + remotes[0].shape[0]
    extra = out_t_ref.shape[1] - hidden
    grads = (edge_grad_ref, out_grad_ref, gain_grad_ref, shift_grad_ref)
    bases = (0, 256, 512, 640)

    @pl.when(number == 0)
    def _():
        for ref, base in zip(grads, bases):
            if first_call:
                ref[...] = jnp.zeros_like(ref)
            else:
                ref[...] = start_ref[:, base : base + ref.shape[1]]
        gain_ref[...] = jnp.broadcast_to(column_ref[:, 1:2], gain_ref.shape)
        shift_ref[...] = jnp.broadcast_to(column_ref[:, 2:3], shift_ref.shape)

    for spot in range(calls):

        @pl.when(number == spot)
        def _(spot=spot):
            remote = dot_nt(turned_ref[:, width : 2 * width], remotes[spot][...])
            term = jnp.concatenate([terms[spot][:, lanes:].astype(F32), remote], axis=1)
            table_ref[...] = masked_table(turned_ref[:, 2 * width :], term, dead)
            self_ref[...] = terms[spot][:, 0:lanes].astype(F32) + column_ref[:, 0:1]

    table_grad_ref[...] = jnp.zeros_like(table_grad_ref)
    self_grad_ref[...] = jnp.zeros_like(self_grad_ref)
    share = 1.0 / channels
    first = lax.broadcasted_iota(jnp.int32, (extra, lanes), 0) == 0
    spans = [slice(spot * lanes, (spot + 1) * lanes) for spot in range(group)]
    total = lambda value: jnp.sum(value, axis=0, keepdims=True)

    def some(index, carry):
        spots = [index * group + spot for spot in range(group)]
        for spot, span in zip(spots, spans):
            slot_row = slot_ref[0, pl.ds(spot, 1), :]
            operand_ref[0:channels, span] = edge_ref[0, spot]
            operand_ref[channels:, span] = selector(slot_row, pool)
            live = jnp.where(first & (slot_row != dead), 1.0, 0.0)
            out_low_ref[hidden:, span] = live.astype(BF16)
        for span in spans:
            value_ref[:, span] = dot(table_ref[...], operand_ref[:, span])
        for span in spans:
            out, slope = gelu_pair_low(value_ref[:, span] + self_ref[...])
            out_low_ref[0:hidden, span] = out
            slope_ref[:, span] = slope
        for span in spans:
            value_ref[:, span] = dot(out_t_ref[...], out_low_ref[:, span])
        for spot, span in zip(spots, spans):
            value = edge_ref[0, spot].astype(F32) + value_ref[:, span]
            centred = value - total(value) * share
            inverse = lax.rsqrt(total(centred * centred) * share + EPSILON)
            normed = centred * inverse
            gain = gain_ref[...]
            result_ref[0, spot] = (normed * gain + shift_ref[...]).astype(BF16)
            scaled = up_ref[0, spot].astype(F32) * gain
            product = scaled * normed
            product_ref[:, span] = product.astype(BF16)
            mixed = inverse * (scaled - total(scaled) * share - normed * (total(product) * share))
            mixed_ref[:, span] = mixed.astype(BF16)
        for span in spans:
            value_ref[:, span] = dot(out_ref[...], mixed_ref[:, span])
        for span in spans:
            grad = slope_ref[:, span].astype(F32) * value_ref[:, span]
            self_grad_ref[...] += grad
            grad_ref[:, span] = grad.astype(BF16)
        out_grad_ref[...] += dot_nt(mixed_ref[...], out_low_ref[...])
        for spot, span in zip(spots, spans):
            edge = dot(weight_ref[...], grad_ref[:, span])
            part_ref[0, spot] = (mixed_ref[:, span].astype(F32) + edge).astype(BF16)
        table_grad_ref[...] += dot_nt(grad_ref[...], operand_ref[...])
        gain_grad_ref[...] += dot_nt(product_ref[...], jnp.ones((8, group * lanes), BF16))
        for spot in spots:
            shift_grad_ref[...] += dot_nt(up_ref[0, spot], jnp.ones((8, lanes), BF16))
        return carry

    lax.fori_loop(0, steps // group, some, 0)
    edge_grad_ref[...] += table_grad_ref[:, 0:channels]
    for spot in range(calls):

        @pl.when(number == spot)
        def _(spot=spot):
            sums[spot][:, 0:lanes] = self_grad_ref[...].astype(BF16)
            sums[spot][:, lanes:] = table_grad_ref[:, channels:].astype(BF16)

    @pl.when(number == calls - 1)
    def _():
        for ref, base in zip(grads, bases):
            total_ref[:, base : base + ref.shape[1]] = ref[...]


def return_body(perm_ref, *refs, count):
    sums = refs[:count]
    turned_ref, up_ref, low_ref, arrive_ref, grad_ref, column_ref = refs[count : count + 6]
    second_ref, leave_ref, mine_ref, other_ref, whole_ref = refs[count + 6 :]
    total = sums[0][...].astype(F32)
    for spot in range(1, count):
        total = total + sums[spot][...].astype(F32)
    low = total.astype(BF16)
    lanes, width = second_ref.shape
    back = dot_tn(low[:, lanes:], turned_ref[:, width : 2 * width])
    leave_ref[...] = back[lanes:].astype(BF16)
    second_ref[...] = (
        up_ref[0].astype(F32) + dot_tn(low[:, 0:lanes], turned_ref[:, 0:width]) + back[0:lanes]
    )
    channels = grad_ref.shape[0]
    hidden = low.shape[0]
    rows = jnp.concatenate([low_ref[...], arrive_ref[...]], axis=0)
    lane = lax.broadcasted_iota(jnp.int32, (channels, 128), 1)
    vectors = jnp.where(
        lane == 0,
        jnp.sum(total[:, 0:lanes], axis=1, keepdims=True),
        jnp.where(
            lane == 1,
            grad_ref[:, 512:513] / column_ref[:, 1:2],
            jnp.where(lane == 2, grad_ref[:, 640:641], grad_ref[:, 256 + hidden : 257 + hidden]),
        ),
    )
    whole_ref[...] = jnp.concatenate(
        [
            dot(low[:, 0:lanes], low_ref[...]),
            dot(low[:, lanes:], rows),
            grad_ref[:, 0:channels],
            grad_ref[:, 256 : 256 + hidden],
            vectors,
        ],
        axis=1,
    )
    core = perm_ref[count + 1]
    half = mine_ref.shape[0]
    mine_ref[...] = whole_ref[pl.ds(pl.multiple_of(core * half, 8), half), :]
    other_ref[...] = whole_ref[pl.ds(pl.multiple_of((1 - core) * half, 8), half), :].astype(BF16)


def backward_body(*refs, count):
    second_ref, return_ref, send_ref, one_ref, two_ref, share_ref, vector_ref, slope_ref = refs[:8]
    blocks = list(refs[8 : 8 + count])
    blocks = blocks + [refs[8 + count].at[spot] for spot in range(count)]
    aggregate_ref, forward_ref, sum_ref, grad_ref = refs[9 + count :]
    lanes = one_ref.shape[0]
    second_grad = second_ref[...] + dot_tn(send_ref[...], return_ref[...])
    _, first_normed, first_inverse = norm_forward(
        one_ref[...], vector_ref[2:3, :], vector_ref[4:5, :]
    )
    _, second_normed, second_inverse = norm_forward(
        two_ref[...], vector_ref[3:4, :], vector_ref[5:6, :]
    )
    total = lambda value: jnp.sum(value, axis=0, keepdims=True)
    grad_ref[3:4, :] = total(second_grad * second_normed)
    grad_ref[5:6, :] = total(second_grad)
    sum_two = norm_backward(second_grad, second_normed, second_inverse, vector_ref[3:4, :])
    low = sum_two.astype(BF16)
    forward_ref[0:lanes, :] = low
    grad_ref[1:2, :] = total(low.astype(F32))
    first_grad = sum_two
    for spot in range(2 * count):
        block = blocks[spot]
        half = (block.shape[0] - 16) // 2
        slope = slope_ref[:, spot * half : (spot + 1) * half].astype(F32)
        grad = (slope * dot_nt(low, block[half : 2 * half, :])).astype(BF16)
        first_grad = first_grad + dot(grad, block[0:half, :])
    grad_ref[2:3, :] = total(first_grad * first_normed)
    grad_ref[4:5, :] = total(first_grad)
    sum_one = norm_backward(first_grad, first_normed, first_inverse, vector_ref[2:3, :])
    sum_ref[...] = sum_one
    aggregate = sum_one.astype(BF16)
    aggregate_ref[...] = aggregate
    grad_ref[0:1, :] = total(share_ref[:, 0:1] * aggregate.astype(F32))
    grad_ref[6:16, :] = jnp.zeros((10, grad_ref.shape[1]), F32)
    forward_ref[lanes:, :] = grad_ref[...].astype(BF16)


def message_backward_body(perm_ref, *refs, count, calls, first_call):
    edge_ref, slot_ref, slope_ref, part_ref, edge_weight_ref, scale_ref = refs[:6]
    weights = refs[6 : 6 + count]
    others = refs[6 + count : 6 + 2 * count]
    ups = refs[6 + 2 * count : 6 + 2 * count + calls]
    refs = refs[6 + 2 * count + calls :]
    if not first_call:
        node_ref, arrive_ref, own_node_ref, own_arrive_ref, mean_ref, own_mean_ref = refs[:6]
        own_up_ref, own_low_ref, own_edge_ref = refs[6:9]
        refs = refs[10:]
    grad_ref = refs[0]
    backs = refs[1 : 1 + calls]
    low_out_ref, edge_out_ref = refs[1 + calls : 3 + calls]
    weight_ref, up_ref, table_grad_ref, self_grad_ref = refs[3 + calls : 7 + calls]
    operand_ref, grad_low_ref = refs[7 + calls : 9 + calls]
    if not first_call:
        mine_ref, other_ref = low_out_ref, edge_out_ref
        low_ref, row_ref, mean_all_ref, up_all_ref = refs[9 + calls : 13 + calls]
        edge_total_ref, bias_ref, total_ref, out_total_ref = refs[13 + calls :]
    group = operand_ref.shape[1] // edge_ref.shape[3]
    number = pl.program_id(0)
    steps, channels, lanes = edge_ref.shape[1:]
    part = 2 * weights[0].shape[0]
    hidden = part * count
    width = backs[0].shape[1]
    pool = backs[0].shape[0]

    @pl.when(number == 0)
    def _():
        fill_weights(perm_ref, weights, others, weight_ref, count)
        if not first_call:
            low_ref[:, 0:pool] = own_low_ref[...]
            row_ref[0:lanes, :] = own_node_ref[0]
            row_ref[lanes:pool, :] = own_arrive_ref[...].reshape(-1, width)
            mean_all_ref[:, 0:lanes] = own_mean_ref[0]
            up_all_ref[0:lanes, :] = own_up_ref[...]
            edge_total_ref[...] = own_edge_ref[...]

    for spot in range(calls):

        @pl.when(number == spot)
        def _(spot=spot):
            value = dot_nt(weight_ref[:, 2 * width : 3 * width], ups[spot][...])
            up_ref[...] = (value * scale_ref[0]).astype(BF16)
            if not first_call:
                at = (spot + 1) * pool
                row_ref[at : at + lanes, :] = node_ref[0]
                row_ref[at + lanes : at + pool, :] = arrive_ref[...].reshape(-1, width)
                at = (spot + 1) * lanes
                mean_all_ref[:, at : at + lanes] = mean_ref[0]
                up_all_ref[at : at + lanes, :] = ups[spot][...]

    table_grad_ref[...] = jnp.zeros_like(table_grad_ref)
    self_grad_ref[...] = jnp.zeros_like(self_grad_ref)
    spans = [slice(spot * lanes, (spot + 1) * lanes) for spot in range(group)]

    def some(index, carry):
        spots = [index * group + spot for spot in range(group)]
        for spot, span in zip(spots, spans):
            operand_ref[0:channels, span] = edge_ref[0, spot]
            operand_ref[channels:, span] = selector(slot_ref[0, pl.ds(spot, 1), :], pool)
        total = self_grad_ref[...]
        for spot, span in zip(spots, spans):
            grad = slope_ref[0, spot] * up_ref[...]
            grad_low_ref[:, span] = grad
            total = total + grad.astype(F32)
        self_grad_ref[...] = total
        for spot, span in zip(spots, spans):
            edge = dot(edge_weight_ref[...], grad_low_ref[:, span])
            grad_ref[0, spot] = (part_ref[0, spot].astype(F32) + edge).astype(BF16)
        table_grad_ref[...] += dot_nt(grad_low_ref[...], operand_ref[...])
        return carry

    lax.fori_loop(0, steps // group, some, 0)
    self_low = self_grad_ref[...].astype(BF16)
    pool_low = table_grad_ref[:, channels:].astype(BF16)
    self_back = dot_tn(self_low, weight_ref[:, 0:width])
    pool_back = dot_tn(pool_low, weight_ref[:, width : 2 * width])
    low_both = jnp.concatenate(
        [
            jnp.concatenate([self_low, jnp.zeros((hidden, pool - lanes), BF16)], axis=1),
            pool_low,
        ],
        axis=0,
    )
    for spot in range(calls):

        @pl.when(number == spot)
        def _(spot=spot):
            backs[spot][0:lanes, :] = (self_back + pool_back[0:lanes]).astype(BF16)
            backs[spot][lanes:, :] = pool_back[lanes:].astype(BF16)
            if not first_call:
                low_ref[:, (spot + 1) * pool : (spot + 2) * pool] = low_both

    if first_call:
        low_out_ref[...] = low_both
        edge_out_ref[...] = table_grad_ref[:, 0:channels]
        return
    edge_total_ref[...] += table_grad_ref[:, 0:channels]

    @pl.when(number == calls - 1)
    def _():
        total_ref[...] = dot(low_ref[...], row_ref[...])
        out_total_ref[...] = dot(mean_all_ref[...], up_all_ref[...])
        ones = jnp.ones((row_ref.shape[0], 128), BF16)
        bias_ref[...] = dot(low_ref[0:hidden, :], ones)
        core = perm_ref[count + 1]
        half = part // 2
        for spot in range(count):
            for place, ref in ((core, mine_ref), (1 - core, other_ref)):
                first = pl.multiple_of(spot * part + place * half, half)
                kind = ref.dtype
                ref[spot, :, 0:width] = total_ref[pl.ds(first, half), :].astype(kind)
                ref[spot, :, width : 2 * width] = total_ref[pl.ds(hidden + first, half), :].astype(kind)
                ref[spot, :, 2 * width : 3 * width] = out_total_ref[pl.ds(first, half), :].astype(kind)
                both = jnp.concatenate(
                    [
                        edge_total_ref[pl.ds(first, half), :],
                        bias_ref[pl.ds(first, half), 0 : ref.shape[2] - 3 * width - channels],
                    ],
                    axis=1,
                )
                ref[spot, :, 3 * width :] = both.astype(kind)


def wide_body(
    perm_ref, low_ref, forward_ref, weight_ref, bias_ref, output_ref, mine_ref, other_ref, all_ref, *, count
):
    width = low_ref.shape[1]
    wide = weight_ref.shape[1]
    step = forward_ref.shape[0] // count
    lanes = step - 16
    low = low_ref[...]
    forward = jnp.concatenate(
        [forward_ref[spot * step : spot * step + lanes, :] for spot in range(count)], axis=0
    )
    lines = None
    for spot in range(count):
        line = forward_ref[spot * step + lanes : (spot + 1) * step, :].astype(F32)
        lines = line if spot == 0 else lines + line
    pre = dot(low, weight_ref[...]) + bias_ref[0:1, :].astype(F32)
    out, slope = gelu_pair(pre)
    grad = slope * dot_nt(forward, output_ref[...])
    all_ref[0:width, :] = dot_tn(low, grad.astype(BF16))
    all_ref[width : width + wide, :] = dot_tn(out.astype(BF16), forward)
    at = width + wide
    total = jnp.broadcast_to(jnp.sum(grad, axis=0, keepdims=True), (8, wide))
    all_ref[at : at + 8, :] = total
    all_ref[at + 8 : at + 16, :] = lines[0:8]
    all_ref[at + 16 :, :] = jnp.zeros((all_ref.shape[0] - at - 16, width), F32)
    half = mine_ref.shape[0]
    core = perm_ref[count + 1]
    mine_ref[...] = all_ref[pl.ds(pl.multiple_of(core * half, 8), half), :]
    other_ref[...] = all_ref[pl.ds(pl.multiple_of((1 - core) * half, 8), half), :].astype(BF16)


def wide_finish_body(
    perm_ref, mine_ref, other_ref, in_ref, out_ref, bias_ref, one_ref, two_ref, three_ref, all_ref, *, count
):
    core = perm_ref[count + 1]
    half = mine_ref.shape[0]
    all_ref[pl.ds(pl.multiple_of(core * half, 8), half), :] = mine_ref[...].astype(F32)
    all_ref[pl.ds(pl.multiple_of((1 - core) * half, 8), half), :] = other_ref[...].astype(F32)
    width = in_ref.shape[0]
    wide = out_ref.shape[0]
    in_ref[...] = all_ref[0:width, :]
    out_ref[...] = all_ref[width : width + wide, :]
    at = width + wide
    bias_ref[...] = all_ref[at : at + 1, :]
    one_ref[...] = all_ref[at + 8 : at + 10, :]
    two_ref[...] = all_ref[at + 10 : at + 12, :]
    three_ref[...] = all_ref[at + 12 : at + 14, :]


def late_finish_body(
    perm_ref,
    mine_ref,
    other_ref,
    mine_parts_ref,
    other_parts_ref,
    nodes_ref,
    output_ref,
    bias_ref,
    turned_ref,
    update_ref,
    hidden_bias_ref,
    gain_ref,
    shift_ref,
    branch_ref,
    edge_ref,
    own_ref,
    whole_ref,
    edges_ref,
    *,
    count,
):
    core = perm_ref[count + 1]
    part = own_ref.shape[0]
    half = part // 2
    width = output_ref.shape[1]
    rows = whole_ref.shape[0] // count // 2
    channels = edges_ref.shape[1]
    for place, ref, parts in ((core, mine_ref, mine_parts_ref), (1 - core, other_ref, other_parts_ref)):
        own_ref[pl.ds(pl.multiple_of(place * half, 8), half), :] = ref[...].astype(F32)
        for spot in range(count):
            value = parts[spot].astype(F32)
            start = pl.multiple_of((place * count + perm_ref[spot]) * rows, 8)
            whole_ref[pl.ds(start, rows), :] = value[0:rows, :]
            first = perm_ref[spot] * part + place * half
            for turn in range(half // 8):
                start = pl.multiple_of(first + 8 * turn, 8)
                edges_ref[pl.ds(start, 8), :] = value[rows:, turn * channels : (turn + 1) * channels]
    nodes_ref[0] = own_ref[:, 0:width].T
    nodes_ref[1] = own_ref[:, width : 2 * width].T
    output_ref[...] = own_ref[:, 2 * width : 3 * width]
    last = own_ref.shape[1]
    bias_ref[...] = own_ref[:, last - 128 :].T[127:128, :]
    end = turned_ref.shape[1]
    hidden = update_ref.shape[0]
    turned_ref[...] = whole_ref[:, 0:end]
    update_ref[...] = whole_ref[:, end : end + hidden].T
    vectors = whole_ref[:, end + hidden :].T
    hidden_bias_ref[...] = vectors[0:1, :]
    gain_ref[...] = vectors[1:2, :]
    shift_ref[...] = vectors[2:3, :]
    branch_ref[...] = vectors[3:4, :]
    edge_ref[...] = edges_ref[...].T


def place_body(perm_ref, *refs, count):
    for spot in range(count):

        @pl.when(pl.program_id(0) == spot)
        def _(spot=spot):
            refs[count][0] = refs[spot][...]


def group_of(total):
    for size in (5, 4, 3, 2, 1):
        if total % size == 0:
            return size


def call(body, grid, ins, outs, scratch, flops, moved, name, perm=None, limit=56, aliases=()):
    whole = lambda block: (block, lambda *_: (0,) * len(block))
    in_specs = [
        pl.BlockSpec(memory_space=pl.ANY)
        if len(entry) == 2
        else pl.BlockSpec(*(entry[1:] if len(entry) == 3 else whole(entry[0].shape)))
        for entry in ins
    ]
    out_specs = [
        pl.BlockSpec(*(entry[2:] if len(entry) == 4 else whole(entry[0]))) for entry in outs
    ]
    spec = pltpu.PrefetchScalarGridSpec(
        num_scalar_prefetch=0 if perm is None else 1,
        grid=grid,
        in_specs=in_specs,
        out_specs=out_specs,
        scratch_shapes=scratch,
    )
    operands = [entry[0] for entry in ins]
    return pl.pallas_call(
        body,
        grid_spec=spec,
        out_shape=[(pltpu.HBM if name in PINNED else jax.ShapeDtypeStruct)(entry[0], entry[1]) for entry in outs],
        input_output_aliases={source + 1: target for source, target in aliases},
        compiler_params=pltpu.CompilerParams(
            dimension_semantics=("arbitrary",) * len(grid), vmem_limit_bytes=limit * 2**20
        ),
        cost_estimate=pl.CostEstimate(flops=flops, bytes_accessed=moved, transcendentals=0),
        name=name,
    )(*([] if perm is None else [perm]), *operands)


def build(prot_size, res_size, mp_size):
    def across(value, offset):
        pairs = [(spot, spot ^ offset) for spot in range(mp_size)]
        return lax.ppermute(value, "mp", pairs)

    def gather(value):
        return [value] + [across(value, offset) for offset in range(1, mp_size)]

    def scatter(parts):
        return [parts[0]] + [across(parts[offset], offset) for offset in range(1, mp_size)]

    def exchange(value):
        return lax.all_to_all(value, "res", split_axis=0, concat_axis=0, tiled=True)

    def block_parts(value):
        place = lax.axis_index("res")
        piece = value.shape[0] // res_size
        parts = [lax.dynamic_slice_in_dim(value, place * piece, piece, 0)]
        low = value.astype(BF16)
        for hop in range(1, res_size):
            target = lax.rem(place + hop, res_size)
            part = lax.dynamic_slice_in_dim(low, target * piece, piece, 0)
            pairs = [(spot, (spot + hop) % res_size) for spot in range(res_size)]
            parts.append(lax.ppermute(part, "res", pairs))
        return parts

    def block_gather(own):
        parts = [own]
        for hop in range(1, res_size):
            pairs = [(spot, (spot - hop) % res_size) for spot in range(res_size)]
            parts.append(lax.ppermute(own, "res", pairs))
        return parts

    def block_order(parts):
        place = lax.axis_index("res")
        piece = parts[0].shape[0]
        both = jnp.concatenate(parts + parts, axis=0)
        return lax.dynamic_slice_in_dim(both, (res_size - place) * piece, res_size * piece, 0)

    def swap(value):
        return lax.ppermute(value, "prot", [(0, 1), (1, 0)])

    def per_device(
        node_states,
        edge_states,
        neighbour_slots,
        send_rows,
        live_counts,
        message_nodes,
        message_edges,
        message_bias,
        message_output,
        feedforward_weight,
        feedforward_bias,
        feedforward_output,
        output_biases,
        norm_gains,
        norm_shifts,
        update_weight,
        update_bias,
        update_output,
        branch_bias,
        edge_gain,
        edge_shift,
        node_cotangent,
        edge_cotangent,
    ):
        proteins, lanes, width = node_states.shape
        own_k, channels = edge_states.shape[2:]
        slots = send_rows.shape[3]
        remote = res_size * slots
        pool = lanes + remote
        part = message_nodes.shape[2]
        hidden = part * mp_size
        update_hidden = update_output.shape[0]
        wide = feedforward_weight.shape[1]
        assert proteins == mp_size and prot_size == 2
        me = lax.axis_index("mp")
        core = lax.axis_index("prot")
        place = lax.axis_index("res")
        dead = lanes + place * slots
        order = [me ^ offset for offset in range(mp_size)]
        perm = jnp.stack(order + [dead, core]).astype(jnp.int32)

        def reorder(value, axis=0):
            size = value.shape[axis] // mp_size
            return jnp.concatenate(
                [lax.dynamic_slice_in_dim(value, spot * size, size, axis) for spot in order], axis=axis
            )

        send_flat = send_rows.reshape(proteins, -1)
        message_pack, leaving = call(
            functools.partial(pack_body, count=mp_size),
            (1,),
            [
                (message_nodes,),
                (message_output,),
                (message_bias,),
                (send_flat,),
                (node_states,),
            ],
            [
                ((part // 2, 3 * width + 128), BF16),
                ((res_size, proteins, slots, width), BF16),
            ],
            [pltpu.VMEM((part, 3 * width + 128), BF16)],
            0,
            0,
            "pack",
            perm,
        )
        arriving = exchange(leaving)
        weights = gather(message_pack)
        other_weights = [swap(value) for value in weights]
        own_slots = lax.dynamic_slice_in_dim(neighbour_slots, me * own_k, own_k, 2)
        alive = lax.broadcasted_iota(jnp.int32, own_slots.shape, 2) + me * own_k < live_counts[..., None]
        own_slots = jnp.transpose(jnp.where(alive, own_slots, dead), (0, 2, 1))
        counts = live_counts.astype(F32)
        scale = (1.0 / jnp.maximum(counts, 1.0))[:, None, :]
        edges = jnp.transpose(edge_states, (0, 2, 3, 1))
        edge_up = jnp.transpose(edge_cotangent, (0, 2, 3, 1))
        turned = update_weight.T
        small = call(
            functools.partial(prepare_body, count=mp_size),
            (1,),
            [
                (message_edges,),
                (turned,),
                (update_output,),
                (update_bias,),
                (edge_gain,),
                (edge_shift,),
                (branch_bias,),
                (feedforward_bias,),
                (output_biases,),
                (norm_gains,),
                (norm_shifts,),
                (live_counts,),
                (send_flat,),
                (node_states, (1, lanes, width), lambda p, perm: (perm[0], 0, 0)),
                (node_cotangent, (1, lanes, width), lambda p, perm: (perm[0], 0, 0)),
                (feedforward_weight,),
                (feedforward_output,),
            ],
            [
                ((channels, hidden), BF16),
                ((hidden, channels), BF16),
                ((channels, 128), F32),
                ((channels, update_hidden + 16), BF16),
                ((channels, update_hidden), BF16),
                ((8, width), F32),
                ((lanes, 128), F32),
                ((remote, lanes), BF16),
                ((16, wide), BF16),
                ((1, lanes, width), BF16),
                ((1, lanes, width), BF16),
                ((wide + 16, width), BF16),
            ],
            [],
            0,
            0,
            "prepare",
            perm,
        )
        weights, other_weights, arriving, own_slots, scale, small = lax.optimization_barrier(
            (weights, other_weights, arriving, own_slots, scale, small)
        )
        (
            edge_weight,
            edge_weight_t,
            columns,
            out_t,
            turned_edge,
            vectors,
            share,
            own_table,
            wide_bias,
            own_node,
            own_up,
            block,
        ) = small
        blocks = gather(block)

        depth = channels + pool
        group = group_of(own_k)
        count = proteins * own_k * lanes
        by_step4 = lambda p, perm: (p, 0, 0, 0)
        by_step3 = lambda p, perm: (p, 0, 0)
        others = proteins - 1

        def shifted(start):
            return (
                lambda p, perm: (perm[p + start], 0, 0, 0),
                lambda p, perm: (perm[p + start], 0, 0),
                lambda p, perm: (0, perm[p + start], 0, 0),
            )

        edge_block = (1, own_k, channels, lanes)
        edge_shape = (proteins, own_k, channels, lanes)
        slope_shape = (proteins, own_k, hidden, lanes)
        slope_block = (1, own_k, hidden, lanes)

        def edge_ins(start):
            by_perm4, by_perm3, _ = shifted(start)
            return [(edges, edge_block, by_perm4), (own_slots, (1, own_k, lanes), by_perm3)]

        def row_ins(start):
            _, by_perm3, by_arrive = shifted(start)
            return [
                (node_states, (1, lanes, width), by_perm3),
                (arriving, (res_size, 1, slots, width), by_arrive),
            ]

        def scale_in(start):
            return (scale, (1, 1, lanes), shifted(start)[1])

        def message_forward(start, calls, after):
            slots_after, _ = lax.optimization_barrier((own_slots, after))
            found = call(
                functools.partial(message_forward_body, count=proteins, calls=calls),
                (calls,),
                [edge_ins(start)[0], (slots_after,) + edge_ins(start)[1][1:]]
                + row_ins(start)
                + [(edge_weight_t,), scale_in(start)]
                + [(value,) for value in weights + other_weights],
                [
                    ((calls, own_k, hidden, lanes), BF16, slope_block, by_step4),
                    ((calls, hidden, lanes), BF16, (1, hidden, lanes), by_step3),
                ]
                + [((lanes, width), BF16)] * calls,
                [
                    pltpu.VMEM((hidden, weights[0].shape[1]), BF16),
                    pltpu.VMEM((hidden, depth), BF16),
                    pltpu.VMEM((hidden, lanes), F32),
                    pltpu.VMEM((hidden, lanes), F32),
                    pltpu.VMEM((group, depth, lanes), BF16),
                    pltpu.VMEM((group, hidden, lanes), F32),
                ],
                2 * calls * own_k * lanes * depth * hidden,
                calls * own_k * lanes * (channels + hidden) * 2,
                "message_forward",
                perm,
            )
            return found[0], found[1], list(found[2:])

        slope_others, mean_others, part_others = message_forward(1, others, own_slots)
        slope_own, mean_own, part_own = message_forward(0, 1, part_others[0])
        parts = scatter(part_own + part_others)
        blocks, _ = lax.optimization_barrier((blocks, part_others[0]))
        other_blocks = swap(jnp.stack(blocks))
        one, two, first_low, second_low, leaving, own_term, wide_slope = call(
            functools.partial(forward_body, count=proteins),
            (),
            [(value,) for value in parts]
            + [(own_node,), (share,), (vectors,), (own_table,), (turned,)]
            + [(value,) for value in blocks]
            + [(other_blocks,)],
            [
                ((lanes, width), F32),
                ((lanes, width), F32),
                ((lanes, width), BF16),
                ((lanes, width), BF16),
                ((remote, width), BF16),
                ((update_hidden, 2 * lanes), BF16),
                ((lanes, wide * mp_size), BF16),
            ],
            [],
            4 * lanes * width * wide * mp_size,
            4 * width * wide * mp_size,
            "feed_forward",
            limit=56,
        )

        arrived = exchange(leaving.reshape(res_size, slots, width)).reshape(remote, width)
        joint = own_term.shape[1] == width
        if joint:
            terms = gather(jnp.concatenate([own_term, arrived], axis=0))
            pool_remotes = []
        else:
            terms = gather(own_term)
            pool_remotes = gather(arrived)
        all_low = lax.all_gather(first_low, "mp", axis=0, tiled=True)
        node_result = lax.all_gather(second_low[None], "mp", axis=0, tiled=True)
        turned_width = 2 * width + channels

        def edge_update(start, calls, earlier):
            by_perm4 = shifted(start)[0]
            ins = (
                edge_ins(start)
                + [(edge_up, edge_block, by_perm4)]
                + [(value,) for value in terms[start : start + calls]]
                + [(value,) for value in pool_remotes[start : start + calls]]
                + [(turned,), (columns,), (out_t,), (update_output,), (turned_edge,)]
            )
            aliases = ()
            if earlier is not None:
                ins = ins + [(earlier[1],), (earlier[0], None)]
                aliases = ((len(ins) - 1, 0),)
            found = call(
                functools.partial(
                    update_body,
                    count=proteins,
                    calls=calls,
                    first_call=earlier is None,
                    joint=joint,
                ),
                (calls,),
                ins,
                [
                    (edge_shape, BF16, edge_block, by_perm4),
                    ((calls, own_k, channels, lanes), BF16, edge_block, by_step4),
                ]
                + [((update_hidden, lanes + pool), BF16)] * calls
                + [((update_hidden, 768), F32)],
                [
                    pltpu.VMEM((update_hidden, depth), BF16),
                    pltpu.VMEM((update_hidden, lanes), F32),
                    pltpu.VMEM((update_hidden, depth), F32),
                    pltpu.VMEM((update_hidden, lanes), F32),
                    pltpu.VMEM((channels, 8), F32),
                    pltpu.VMEM((channels, 8), F32),
                    pltpu.VMEM((update_hidden, channels), F32),
                    pltpu.VMEM((channels, update_hidden + 16), F32),
                    pltpu.VMEM((channels, lanes), F32),
                    pltpu.VMEM((channels, lanes), F32),
                    pltpu.VMEM((depth, group * lanes), BF16),
                    pltpu.VMEM((update_hidden + 16, group * lanes), BF16),
                    pltpu.VMEM((channels, group * lanes), BF16),
                    pltpu.VMEM((update_hidden, group * lanes), BF16),
                    pltpu.VMEM((channels, group * lanes), BF16),
                    pltpu.VMEM((update_hidden, group * lanes), F32),
                    pltpu.VMEM((update_hidden, group * lanes), BF16),
                ],
                2 * calls * own_k * lanes * (2 * depth + 4 * channels) * update_hidden,
                calls * own_k * lanes * channels * 8,
                "edge_update",
                perm,
                aliases=aliases,
            )
            return found[0], found[-1], found[1], found[2:-1]

        edge_result, grads, edge_part_own, sums_own = edge_update(0, 1, None)
        edge_result, grads, edge_part_others, sums_others = edge_update(1, others, (edge_result, grads))
        sums_own, sums_others, all_low = lax.optimization_barrier((sums_own, sums_others, all_low))
        sums = scatter(list(sums_own) + list(sums_others))
        whole_width = turned_width + update_hidden + 128
        second_part, leaving, whole_mine, whole_other = call(
            functools.partial(return_body, count=proteins),
            (1,),
            [(value,) for value in sums]
            + [(turned,), (own_up,), (second_low,), (arrived,), (grads,), (columns,)],
            [
                ((lanes, width), F32),
                ((remote, width), BF16),
                ((update_hidden // 2, whole_width), F32),
                ((update_hidden // 2, whole_width), BF16),
            ],
            [pltpu.VMEM((update_hidden, whole_width), F32)],
            2 * (lanes + pool) * width * update_hidden,
            (lanes + pool) * width * 2,
            "update_return",
            perm,
        )
        whole_swapped = swap(whole_other)
        returned = exchange(leaving.reshape(res_size, slots, width)).reshape(remote, width)
        whole = (whole_mine + whole_swapped.astype(F32)).astype(BF16)
        whole, returned = lax.optimization_barrier((whole, returned))
        whole = lax.psum_scatter(whole, "mp", scatter_dimension=0, tiled=True)
        aggregate_grad, forward_grad, sum_one, _ = call(
            functools.partial(backward_body, count=proteins),
            (),
            [(second_part,), (returned,), (own_table,), (one,), (two,), (share,), (vectors,), (wide_slope,)]
            + [(value,) for value in blocks]
            + [(other_blocks,)],
            [
                ((lanes, width), BF16),
                ((lanes + 16, width), BF16),
                ((lanes, width), F32),
                ((16, width), F32),
            ],
            [],
            6 * lanes * width * wide * mp_size,
            4 * width * wide * mp_size,
            "feed_backward",
            limit=56,
        )
        ups = gather(aggregate_grad)
        all_forward = lax.all_gather(forward_grad, "mp", axis=0, tiled=True)
        total_width = 3 * width + -(-(channels + 1) // 128) * 128
        late_shape = (proteins, part // 2, total_width)

        def message_backward(start, calls, earlier):
            by_perm4 = shifted(start)[0]
            ins = (
                edge_ins(start)
                + [
                    (slope_own if earlier is None else slope_others, slope_block, by_step4),
                    (edge_part_own if earlier is None else edge_part_others, edge_block, by_step4),
                    (edge_weight,),
                    scale_in(start),
                ]
                + [(value,) for value in weights + other_weights + ups[start : start + calls]]
            )
            aliases = ()
            scratch = [
                pltpu.VMEM((hidden, weights[0].shape[1]), BF16),
                pltpu.VMEM((hidden, lanes), BF16),
                pltpu.VMEM((hidden, depth), F32),
                pltpu.VMEM((hidden, lanes), F32),
                pltpu.VMEM((depth, group * lanes), BF16),
                pltpu.VMEM((hidden, group * lanes), BF16),
            ]
            if earlier is None:
                last = [((2 * hidden, pool), BF16), ((hidden, channels), F32)]
            else:
                mean_block = (1, hidden, lanes)
                ins = ins + row_ins(start)
                ins = ins + [
                    (node_states, (1, lanes, width), lambda p, perm: (perm[0], 0, 0)),
                    (arriving, (res_size, 1, slots, width), lambda p, perm: (0, perm[0], 0, 0)),
                    (mean_others, mean_block, by_step3),
                    (mean_own,),
                    (ups[0],),
                    (earlier[1],),
                    (earlier[2],),
                    (earlier[0], None),
                ]
                aliases = ((len(ins) - 1, 0),)
                last = [(late_shape, F32), (late_shape, BF16)]
                scratch = scratch + [
                    pltpu.VMEM((2 * hidden, proteins * pool), BF16),
                    pltpu.VMEM((proteins * pool, width), BF16),
                    pltpu.VMEM((hidden, proteins * lanes), BF16),
                    pltpu.VMEM((proteins * lanes, width), BF16),
                    pltpu.VMEM((hidden, channels), F32),
                    pltpu.VMEM((hidden, 128), F32),
                    pltpu.VMEM((2 * hidden, width), F32),
                    pltpu.VMEM((hidden, width), F32),
                ]
            found = call(
                functools.partial(
                    message_backward_body, count=proteins, calls=calls, first_call=earlier is None
                ),
                (calls,),
                ins,
                [(edge_shape, BF16, edge_block, by_perm4)] + [((pool, width), BF16)] * calls + last,
                scratch,
                2 * calls * own_k * lanes * (depth + channels) * hidden,
                calls * own_k * lanes * (3 * channels + hidden) * 2,
                "message_backward",
                perm,
                aliases=aliases,
            )
            return found[0], found[-2], found[-1], found[1 : 1 + calls]

        edge_grad, own_low, own_edge, back_own = message_backward(0, 1, None)
        edge_grad, late_mine, late_other, back_others = message_backward(
            1, others, (edge_grad, own_low, own_edge)
        )
        found = list(back_own) + list(back_others)
        late_swapped = swap(late_other)
        backs, late_mine, all_forward, node_result, whole = lax.optimization_barrier(
            (found, late_mine, all_forward, node_result, whole)
        )
        back = scatter(backs)
        late = late_mine + late_swapped.astype(F32)
        late_own = late[0]
        late_low = [late[offset].astype(BF16) for offset in range(1, mp_size)]
        all_forward, late_own, late_low = lax.optimization_barrier((all_forward, late_own, late_low))
        late_parts = scatter([late_own] + late_low)
        unit = prot_size * res_size * 8
        wide_rows = -(-(width + wide + 16) // unit) * unit
        early_mine, early_other = call(
            functools.partial(wide_body, count=proteins),
            (1,),
            [
                (all_low,),
                (all_forward,),
                (feedforward_weight,),
                (wide_bias,),
                (feedforward_output,),
            ],
            [((wide_rows // 2, width), F32), ((wide_rows // 2, width), BF16)],
            [pltpu.VMEM((wide_rows, width), F32)],
            10 * proteins * lanes * width * wide,
            8 * proteins * lanes * width,
            "feed_weights",
            perm,
        )
        back, early_other, early_mine = lax.optimization_barrier((back, early_other, early_mine))
        early_swapped = swap(early_other)
        total = sum(value.astype(F32) for value in back)
        leaving = total[lanes:].astype(BF16).reshape(res_size, slots, width)
        leaving, early_swapped = lax.optimization_barrier((leaving, early_swapped))
        early = (early_mine + early_swapped.astype(F32)).astype(BF16)
        early, leaving = lax.optimization_barrier((early, leaving))
        early, whole = lax.psum((early, whole), "res")
        returned = exchange(leaving)
        node_grad = (
            sum_one
            + total[:lanes]
            + jnp.einsum(
                "sr,sd->rd", own_table, returned.reshape(remote, width), preferred_element_type=F32
            )
        ).astype(BF16)
        node_grad, late_parts = lax.optimization_barrier((node_grad, late_parts))
        late = sum(value.astype(F32) for value in late_parts)
        late_parts = block_parts(late)
        node_parts = gather(node_grad)
        late = sum(value.astype(F32) for value in late_parts).astype(BF16)
        late, node_parts = lax.optimization_barrier((late, node_parts))
        late_parts = block_gather(late)
        (node_grad,) = call(
            functools.partial(place_body, count=proteins),
            (proteins,),
            [(value,) for value in node_parts],
            [((proteins, lanes, width), BF16, (1, lanes, width), shifted(0)[1])],
            [],
            0,
            4 * proteins * lanes * width,
            "place_rows",
            perm,
        )
        early, whole, node_grad, late_parts = lax.optimization_barrier(
            (early, whole, node_grad, late_parts)
        )
        late = block_order(late_parts)
        early_swapped = swap(early)
        late_swapped = swap(late)
        fold = late[:, 3 * width : 3 * width + channels].reshape(-1, 8, channels)
        fold = jnp.transpose(fold, (1, 0, 2)).reshape(8, -1)
        shared_parts = gather(jnp.concatenate([whole, fold], axis=0))
        weight_in_grad, weight_out_grad, wide_bias_grad, biases_grad, gains_grad, shifts_grad = call(
            functools.partial(wide_finish_body, count=proteins),
            (1,),
            [(early,), (early_swapped,)],
            [
                ((width, wide), F32),
                ((wide, width), F32),
                ((1, wide), F32),
                ((2, width), F32),
                ((2, width), F32),
                ((2, width), F32),
            ],
            [pltpu.VMEM((wide_rows, width), F32)],
            0,
            8 * wide_rows * width,
            "feed_weights_out",
            perm,
        )
        weight_in_grad, shared_parts, late_swapped = lax.optimization_barrier(
            (weight_in_grad, shared_parts, late_swapped)
        )
        shared = jnp.stack(shared_parts)
        found = call(
            functools.partial(late_finish_body, count=proteins),
            (1,),
            [(late,), (late_swapped,), (shared,), (swap(shared),)],
            [
                ((2, width, part), F32),
                ((part, width), F32),
                ((1, part), F32),
                ((update_hidden, turned_width), F32),
                ((update_hidden, channels), F32),
                ((1, update_hidden), F32),
                ((1, channels), F32),
                ((1, channels), F32),
                ((1, channels), F32),
                ((channels, hidden), F32),
            ],
            [
                pltpu.VMEM((part, total_width), F32),
                pltpu.VMEM((update_hidden, turned_width + update_hidden + 128), F32),
                pltpu.VMEM((hidden, channels), F32),
            ],
            0,
            8 * hidden * total_width,
            "message_weights_out",
            perm,
            16,
        )
        turn = lambda value: jnp.transpose(value, (0, 3, 1, 2))
        return (
            node_result,
            turn(edge_result),
            node_grad,
            turn(edge_grad),
            found[0],
            found[9],
            found[2].reshape(part),
            found[1],
            weight_in_grad,
            wide_bias_grad.reshape(wide),
            weight_out_grad,
            biases_grad,
            gains_grad,
            shifts_grad,
            found[3].T,
            found[5].reshape(update_hidden),
            found[4],
            found[8].reshape(channels),
            found[6].reshape(channels),
            found[7].reshape(channels),
        )

    return per_device


def solution(mesh):
    return jax.shard_map(
        build(mesh.shape["prot"], mesh.shape["res"], mesh.shape["mp"]),
        mesh=mesh,
        in_specs=(
            P("prot", "res", None),
            P("prot", "res", "mp", None),
            P("prot", "res", None),
            P("prot", "res", None, None),
            P("prot", "res"),
            P(None, None, "mp"),
            P(),
            P("mp"),
            P("mp", None),
            P(None, "mp"),
            P("mp"),
            P("mp", None),
            P(),
            P(),
            P(),
            P(),
            P(),
            P(),
            P(),
            P(),
            P(),
            P("prot", "res", None),
            P("prot", "res", "mp", None),
        ),
        out_specs=(
            P("prot", "res", None),
            P("prot", "res", "mp", None),
            P("prot", "res", None),
            P("prot", "res", "mp", None),
            P(None, None, "mp"),
            P(),
            P("mp"),
            P("mp", None),
            P(None, "mp"),
            P("mp"),
            P("mp", None),
            P(),
            P(),
            P(),
            P(),
            P(),
            P(),
            P(),
            P(),
            P(),
        ),
        check_vma=False,
    )
```

profile of v0, /device:TPU:0, one launch (start us, length us, event | category | flops | bytes accessed | tf_op | source)
XLA Modules:
  0.0 316.7 jit_solution(5122599996587497030)
XLA Ops:
  7.2 1.4 reshape.89.send_ref
  9.2 3.4 %pack.1 = (bf16[64,1664]{1,0:T(8,128)(2,1)}, bf16[4,4,16,512]{3,2,1,0:T(8,128)(2,1)}) custom-call(s32[6]{0:T(128)} %stack.57.perm_ref, bf16[2,512,128]{2,1,0:T(8,128)(2,1)} %nodes_ref.1, bf16[128,512]{1,0:T(8,128)(2,1)} %output_ref.2, bf16[128]{0:T(256)(128)(2,1)} %bias_ref.1, s32[4,64]{1,0:T(4,128)} %reshape.89.send_ref, bf16[4,256,512]{2,1,0:T(8,128)(2,1)} %refs_19_.1), custom_call_target="tpu_custom_call" | custom-call | tf_op jit(solution)/shard_map/pack/pallas_call | solution.py:750
  12.6 2.9 collective-permute-start
  15.6 1.5 collective-permute-start.1
  17.1 5.3 %all-to-all-start = ((bf16[4,4,16,512]{3,2,1,0:T(8,128)(2,1)}), bf16[4,4,16,512]{3,2,1,0:T(8,128)(2,1)S(1)}, u32[]{:S(2)}, u32[]{:S(2)}) async-start(bf16[4,4,16,512]{3,2,1,0:T(8,128)(2,1)} %get-tuple-element.177), calls=%async_computation | async-start | bytes 524288 | tf_op jit(solution)/shard_map/all_to_all | solution.py:775
  23.8 4.1 %prepare.1 = (bf16[192,512]{1,0:T(8,128)(2,1)}, bf16[512,192]{1,0:T(8,128)(2,1)}, f32[192,128]{1,0:T(8,128)}, bf16[192,208]{1,0:T(8,128)(2,1)}, bf16[192,192]{1,...) custom-call(s32[6]{0:T(128)} %stack.57.perm_ref, ...), custom_call_target="tpu_custom_call" | custom-call | tf_op jit(solution)/shard_map/prepare/pallas_call | solution.py:750
  29.5 2.5 all-to-all-done.refs_3_.refs_18_.refs_20_
  32.1 1.6 collective-permute-start.10
  33.6 1.5 collective-permute-start.11
  35.7 22.5 %message_forward.2 = (bf16[3,15,512,256]{3,2,1,0:T(8,128)(2,1)}, bf16[3,512,256]{2,1,0:T(8,128)(2,1)}, bf16[256,512]{1,0:T(8,128)(2,1)}, bf16[256,512]{1,0:T(8,128)(2,1)}, bf16[256,512]{1,0:T(8,128)(2,1)}) custom-call(s32[6]{0:T(128)} %stack.57.perm_ref, bf16[4,15,192,256]{3,2,1,0:T(8,128)(2,1)} %bitcast.51, s32[4,15,256]{2,1,0:T(8,128)} %fusion.1.refs_1_, ...), custom_call_target="tpu_custom_call" | custom-call | flops 6039797760 | bytes 16220160 | tf_op jit(solution)/shard_map/message_forward/pallas_call | solution.py:750
  59.4 1.5 collective-permute-start.7
  60.9 1.5 collective-permute-start.8
  62.9 10.2 %message_forward.3 = (bf16[1,15,512,256]{3,2,1,0:T(8,128)(2,1)}, bf16[1,512,256]{2,1,0:T(8,128)(2,1)}, bf16[256,512]{1,0:T(8,128)(2,1)}) custom-call(s32[6]{0:T(128)} %stack.57.perm_ref, bf16[4,15,192,256]{3,2,1,0:T(8,128)(2,1)} %bitcast.52, s32[4,15,256]{2,1,0:T(8,128)} %fusion.1.refs_1_, bf16[4,256,512]{2,1,0:T(8,128)(2,1)} %refs_19_.1, ...), custom_call_target="tpu_custom_call" | custom-call | flops 2013265920 | bytes 5406720 | tf_op jit(solution)/shard_map/message_forward/pallas_call | solution.py:750
  73.1 1.8 collective-permute-done.8.refs_2_
  76.4 6.7 %feed_forward.1 = (f32[256,512]{1,0:T(8,128)}, f32[256,512]{1,0:T(8,128)}, bf16[256,512]{1,0:T(8,128)(2,1)}, bf16[256,512]{1,0:T(8,128)(2,1)}, bf16[64,512]{1,0:...) custom-call(bf16[256,512]{1,0:T(8,128)(2,1)} %get-tuple-element.206.refs_0_, ...), custom_call_target="tpu_custom_call" | custom-call | flops 1073741824 | bytes 4194304 | tf_op jit(solution)/shard_map/feed_forward/pallas_call | solution.py:750
  83.2 9.7 %all_to_all.20 = bf16[4,16,512]{2,1,0:T(8,128)(2,1)S(1)} all-to-all(bf16[4,16,512]{2,1,0:T(8,128)(2,1)} %bitcast.80), channel_id=1, replica_groups=mesh['prot'=2,'res'=4,'mp'=4] {'res'}, dimensions={0} | all-to-all | bytes 131072 | tf_op jit(solution)/shard_map/all_to_all | solution.py:775
  92.9 1.0 pad_maximum_fusion.2.refs_3_
  93.9 0.9 collective-permute-start.14
  94.8 1.5 collective-permute-start.15
  96.4 1.1 collective-permute-start.16
  97.5 12.7 %edge_update.2 = (bf16[4,15,192,256]{3,2,1,0:T(8,128)(2,1)}, bf16[1,15,192,256]{3,2,1,0:T(8,128)(2,1)}, bf16[192,576]{1,0:T(8,128)(2,1)}, f32[192,768]{1,0:T(8,128)}) custom-call(s32[6]{0:T(128)} %stack.57.perm_ref, bf16[4,15,192,256]{3,2,1,0:T(8,128)(2,1)} %bitcast.53, s32[4,15,256]{2,1,0:T(8,128)} %fusion.1.refs_1_, bf16[4,15,192,256]{3,2,1,0:T(8,128)(2,1)} %bitcast.62, ...), custom_call_target="tpu_custom_call" | custom-call | flops 2642411520 | bytes 5898240 | tf_op jit(solution)/shard_map/edge_update/pallas_call | solution.py:750
  111.0 31.3 %edge_update.3 = (bf16[4,15,192,256]{3,2,1,0:T(8,128)(2,1)}, bf16[3,15,192,256]{3,2,1,0:T(8,128)(2,1)}, bf16[192,576]{1,0:T(8,128)(2,1)}, bf16[192,576]{1,0:T(8,...) custom-call(s32[6]{0:T(128)} %stack.57.perm_ref, ...), custom_call_target="tpu_custom_call", output_to_operand_aliasing={{0}: (13, {})} | custom-call | flops 7927234560 | bytes 17694720 | tf_op jit(solution)/shard_map/edge_update/pallas_call | solution.py:750
  143.3 1.5 collective-permute-start.18
  144.8 1.1 collective-permute-start.19
  145.9 4.6 %collective-permute-done.17.refs_1_ = bf16[192,576]{1,0:T(8,128)(2,1)S(1)} collective-permute-done((bf16[192,576]{1,0:T(8,128)(2,1)}, bf16[192,576]{1,0:T(8,128)(2,1)S(1)}, u32[]{:S(2)}, u32[]{:S(2)}) %collective-permute-start.17) | collective-permute-done | bytes 221216 | tf_op jit(solution)/shard_map/ppermute | solution.py:766
  150.5 3.2 %collective-permute-done.18.refs_2_ = bf16[192,576]{1,0:T(8,128)(2,1)S(1)} collective-permute-done((bf16[192,576]{1,0:T(8,128)(2,1)}, bf16[192,576]{1,0:T(8,128)(2,1)S(1)}, u32[]{:S(2)}, u32[]{:S(2)}) %collective-permute-start.18) | collective-permute-done | bytes 221216 | tf_op jit(solution)/shard_map/ppermute | solution.py:766
  154.5 4.0 %update_return.1 = (f32[256,512]{1,0:T(8,128)}, bf16[64,512]{1,0:T(8,128)(2,1)}, f32[96,1536]{1,0:T(8,128)}, bf16[96,1536]{1,0:T(8,128)(2,1)}) custom-call(s32[6]{0:T(128)} %stack.57.perm_ref, bf16[192,576]{1,0:T(8,128)(2,1)} %get-tuple-element.232.refs_0_, bf16[192,576]{1,0:T(8,128)(2,1)} %copy-done.35, bf16[192,576]{1,0:T(8,128)(2,1)} %copy-done.36, ...), custom_call_target="tpu_custom_call" | custom-call | flops 113246208 | bytes 589824 | tf_op jit(solution)/shard_map/update_return/pallas_call | solution.py:750
  158.5 4.0 %all-to-all-start.2 = ((bf16[4,16,512]{2,1,0:T(8,128)(2,1)}), bf16[4,16,512]{2,1,0:T(8,128)(2,1)S(1)}, u32[]{:S(2)}, u32[]{:S(2)}) async-start(bf16[4,16,512]{2,1,0:T(8,128)(2,1)} %bitcast.79), calls=%async_computation.2 | async-start | bytes 131072 | tf_op jit(solution)/shard_map/all_to_all | solution.py:775
  162.5 1.8 add_convert_fusion.1
  164.3 3.9 %all-to-all-done.2 = bf16[4,16,512]{2,1,0:T(8,128)(2,1)S(1)} async-done(((bf16[4,16,512]{2,1,0:T(8,128)(2,1)}), bf16[4,16,512]{2,1,0:T(8,128)(2,1)S(1)}, u32[]{:S(2)}, u32[]{:S(2)}) %all-to-all-start.2) | async-done | bytes 65568 | tf_op jit(solution)/shard_map/all_to_all | solution.py:775
  168.9 6.2 %feed_backward.1 = (bf16[256,512]{1,0:T(8,128)(2,1)}, bf16[272,512]{1,0:T(8,128)(2,1)}, f32[256,512]{1,0:T(8,128)}, f32[16,512]{1,0:T(8,128)}) custom-call(f32[256,512]{1,0:T(8,128)} %get-tuple-element.239.refs_0_, bf16[64,512]{1,0:T(8,128)(2,1)} %bitcast.73, bf16[64,256]{1,0:T(8,128)(2,1)} %get-tuple-element.212.refs_7_.refs_2_, ...), custom_call_target="tpu_custom_call" | custom-call | flops 1610612736 | bytes 4194304 | tf_op jit(solution)/shard_map/feed_backward/pallas_call | solution.py:750
  176.4 2.1 collective-permute-start.23
  178.6 10.4 %message_backward.2 = (bf16[4,15,192,256]{3,2,1,0:T(8,128)(2,1)}, bf16[320,512]{1,0:T(8,128)(2,1)}, bf16[1024,320]{1,0:T(8,128)(2,1)}, f32[512,192]{1,0:T(8,128)}) custom-call(s32[6]{0:T(128)} %stack.57.perm_ref, bf16[4,15,192,256]{3,2,1,0:T(8,128)(2,1)} %bitcast.55, s32[4,15,256]{2,1,0:T(8,128)} %fusion.1.refs_1_, ...), custom_call_target="tpu_custom_call" | custom-call | flops 2768240640 | bytes 8355840 | tf_op jit(solution)/shard_map/message_backward/pallas_call | solution.py:750
  190.3 26.0 %message_backward.3 = (bf16[4,15,192,256]{3,2,1,0:T(8,128)(2,1)}, bf16[320,512]{1,0:T(8,128)(2,1)}, bf16[320,512]{1,0:T(8,128)(2,1)}, bf16[320,512]{1,0:T(8,128)...) custom-call(s32[6]{0:T(128)} %stack.57.perm_ref, ...), custom_call_target="tpu_custom_call", output_to_operand_aliasing={{0}: (27, {})} | custom-call | flops 8304721920 | bytes 25067520 | tf_op jit(solution)/shard_map/message_backward/pallas_call | solution.py:750
  216.5 2.8 all-gather.7.cloned.1.call-done.forward_ref
  219.3 1.5 collective-permute-start.24
  221.3 1.5 collective-permute-start.26
  222.8 1.7 fusion.3
  224.6 7.1 %feed_weights.1 = (f32[544,512]{1,0:T(8,128)}, bf16[544,512]{1,0:T(8,128)(2,1)}) custom-call(s32[6]{0:T(128)} %stack.57.perm_ref, bf16[1024,512]{1,0:T(8,128)(2,1)} %all-gather.5.cloned.1.call-done.low_ref, bf16[1088,512]{1,0:T(8,128)(2,1)} %all-gather.7.cloned.1.call-done.forward_ref, bf16[512,512]{1,0:T(8,128)(2,1)} %weight_ref.1, ...), custom_call_target="tpu_custom_call" | custom-call | flops 2684354560 | bytes 4194304 | tf_op jit(solution)/shard_map/feed_weights/pallas_call | solution.py:750
  231.7 5.4 %collective-permute-done.25 = bf16[320,512]{1,0:T(8,128)(2,1)S(1)} collective-permute-done((bf16[320,512]{1,0:T(8,128)(2,1)}, bf16[320,512]{1,0:T(8,128)(2,1)S(1)}, u32[]{:S(2)}, u32[]{:S(2)}) %collective-permute-start.25) | collective-permute-done | bytes 327712 | tf_op jit(solution)/shard_map/ppermute | solution.py:766
  238.0 1.3 collective-permute-done.28
  239.4 1.0 add_convert_fusion
  240.3 4.6 %all-to-all-start.3 = ((bf16[4,16,512]{2,1,0:T(8,128)(2,1)}), bf16[4,16,512]{2,1,0:T(8,128)(2,1)S(1)}, u32[]{:S(2)}, u32[]{:S(2)}) async-start(bf16[4,16,512]{2,1,0:T(8,128)(2,1)} %bitcast.24), calls=%async_computation.3 | async-start | bytes 131072 | tf_op jit(solution)/shard_map/all_to_all | solution.py:775
  245.5 1.5 collective-permute-start.30
  247.0 1.5 collective-permute-start.31
  248.4 2.2 all-to-all-done.3
  250.9 2.5 collective-permute-done.29
  253.4 4.1 %collective-permute-done.30 = bf16[64,1792]{1,0:T(8,128)(2,1)S(1)} collective-permute-done((bf16[64,1792]{1,0:T(8,128)(2,1)S(1)}, bf16[64,1792]{1,0:T(8,128)(2,1)S(1)}, u32[]{:S(2)}, u32[]{:S(2)}) %collective-permute-start.30) | collective-permute-done | bytes 229408 | tf_op jit(solution)/shard_map/ppermute | solution.py:766
  257.6 3.6 %collective-permute-start.34 = (bf16[16,1792]{1,0:T(8,128)(2,1)S(1)}, bf16[16,1792]{1,0:T(8,128)(2,1)S(1)}, u32[]{:S(2)}, u32[]{:S(2)}) collective-permute-start(bf16[16,1792]{1,0:T(8,128)(2,1)S(1)} %get-tuple-element.342), channel_id=1, source_target_pairs={{0,12},{4,0},{8,4},{12,8},{1,13},{5,1},{9,5},{13,9},{2,14},{6,2},{... | collective-permute-start | bytes 172040 | tf_op jit(solution)/shard_map/ppermute | solution.py:786
  261.2 1.1 collective-permute-start.32
  262.4 1.5 collective-permute-start.35
  265.0 1.5 collective-permute-start.37
  266.4 5.7 %collective-permute-done.33 = bf16[16,1792]{1,0:T(8,128)(2,1)S(1)} collective-permute-done((bf16[16,1792]{1,0:T(8,128)(2,1)S(1)}, bf16[16,1792]{1,0:T(8,128)(2,1)S(1)}, u32[]{:S(2)}, u32[]{:S(2)}) %collective-permute-start.33) | collective-permute-done | bytes 57376 | tf_op jit(solution)/shard_map/ppermute | solution.py:786
  272.2 2.8 collective-permute-done.36.refs_2_
  275.1 2.9 collective-permute-start.38
  279.1 3.4 %place_rows.1 = bf16[4,256,512]{2,1,0:T(8,128)(2,1)} custom-call(s32[6]{0:T(128)} %stack.57.perm_ref, bf16[256,512]{1,0:T(8,128)(2,1)} %copy-done.19, bf16[256,512]{1,0:T(8,128)(2,1)} %copy-done.29, bf16[256,512]{1,0:T(8,128)(2,1)} %copy-done.30, bf16[256,512]{1,0:T(8,128)(2,1)} %copy-done.31), custom_call_target="tpu_custom_call" | custom-call | bytes 2097152 | tf_op jit(solution)/shard_map/place_rows/pallas_call | solution.py:750
  283.2 2.8 collective-permute-done.40
  286.0 9.0 %all-reduce.4.cloned.1.call-done = (bf16[544,512]{1,0:T(8,128)(2,1)}, bf16[24,1536]{1,0:T(8,128)(2,1)}) async-done(((bf16[544,512]{1,0:T(8,128)(2,1)}, bf16[24,1536]{1,0:T(8,128)(2,1)}), (bf16[544,512]{1,0:T(8,128)(2,1)}, bf16[24,1536]{1,0:T(8,128)(2,1)})) %all-reduce.4.cloned.1.call-update) | async-done | bytes 630800 | tf_op jit(solution)/shard_map/psum | solution.py:1259
  296.8 1.3 collective-permute-start.42
  298.1 1.3 collective-permute-start.43
  301.2 3.6 %feed_weights_out.1 = (f32[512,512]{1,0:T(8,128)}, f32[512,512]{1,0:T(8,128)}, f32[1,512]{1,0:T(1,128)}, f32[2,512]{1,0:T(2,128)}, f32[2,512]{1,0:T(2,128)}, /*index=5*/f32[2,512]{1,0:T(2,128)}) custom-call(s32[6]{0:T(128)} %stack.57.perm_ref, bf16[544,512]{1,0:T(8,128)(2,1)} %get-tuple-element.308.mine_ref, bf16[544,512]{1,0:T(8,128)(2,1)} %copy-done.21), custom_call_target="tpu_custom_call" | custom-call | bytes 4456448 | tf_op jit(solution)/shard_map/feed_weights_out/pallas_call | solution.py:750
  305.1 1.7 collective-permute-done.46.other_parts_ref
  306.8 2.4 message_weights_out.1
  309.2 1.0 copy.68
  (193 shorter events, 22.5 us)
Async XLA Ops:
  7.2 20.7 %copy-start = (s32[4,256,60]{1,0,2:T(4,128)S(1)}, s32[4,256,60]{1,0,2:T(4,128)}, u32[]{:S(2)}) copy-start(s32[4,256,60]{1,0,2:T(4,128)} %param.25) | copy-start | bytes 737284
  12.6 15.3 %collective-permute-start = (bf16[64,1664]{1,0:T(8,128)(2,1)}, bf16[64,1664]{1,0:T(8,128)(2,1)S(1)}, u32[]{:S(2)}, u32[]{:S(2)}) collective-permute-start(bf16[64,1664]{1,0:T(8,128)(2,1)} %get-tuple-element.195.refs_6_), channel_id=1, source_target_pairs={{0,1},{1,0},{2,3},{3,2},{4,5},{5,4},{6,7},{7,6},{8,9},{9,8},{10,11... | collective-permute-start | bytes 638984 | tf_op jit(solution)/shard_map/ppermute | solution.py:766
  15.6 12.7 %collective-permute-start.1 = (bf16[64,1664]{1,0:T(8,128)(2,1)}, bf16[64,1664]{1,0:T(8,128)(2,1)S(1)}, u32[]{:S(2)}, u32[]{:S(2)}) collective-permute-start(bf16[64,1664]{1,0:T(8,128)(2,1)} %get-tuple-element.195.refs_6_), channel_id=1, source_target_pairs={{0,2},{1,3},{2,0},{3,1},{4,6},{5,7},{6,4},{7,5},{8,10},{9,11},{10,... | collective-permute-start | bytes 638984 | tf_op jit(solution)/shard_map/ppermute | solution.py:766
  17.1 11.5 %collective-permute-start.2 = (bf16[64,1664]{1,0:T(8,128)(2,1)}, bf16[64,1664]{1,0:T(8,128)(2,1)S(1)}, u32[]{:S(2)}, u32[]{:S(2)}) collective-permute-start(bf16[64,1664]{1,0:T(8,128)(2,1)} %get-tuple-element.195.refs_6_), channel_id=1, source_target_pairs={{0,3},{1,2},{2,1},{3,0},{4,7},{5,6},{6,5},{7,4},{8,11},{9,10},{10,... | collective-permute-start | bytes 638984 | tf_op jit(solution)/shard_map/ppermute | solution.py:766
  17.1 12.4 %collective-permute-start.3 = (bf16[64,1664]{1,0:T(8,128)(2,1)}, bf16[64,1664]{1,0:T(8,128)(2,1)S(1)}, u32[]{:S(2)}, u32[]{:S(2)}) collective-permute-start(bf16[64,1664]{1,0:T(8,128)(2,1)} %get-tuple-element.195.refs_6_), channel_id=1, source_target_pairs={{0,16},{16,0},{1,17},{17,1},{2,18},{18,2},{3,19},{19,3},{4,20},{20... | collective-permute-start | bytes 638984 | tf_op jit(solution)/shard_map/ppermute | solution.py:803
  17.1 14.9 %all-to-all-start = ((bf16[4,4,16,512]{3,2,1,0:T(8,128)(2,1)}), bf16[4,4,16,512]{3,2,1,0:T(8,128)(2,1)S(1)}, u32[]{:S(2)}, u32[]{:S(2)}) async-start(bf16[4,4,16,512]{3,2,1,0:T(8,128)(2,1)} %get-tuple-element.177), calls=%async_computation | async-start | bytes 524288 | tf_op jit(solution)/shard_map/all_to_all | solution.py:775
  22.5 119.9 %all-gather.5.cloned.1.call-start = ((), (), s32[]{:S(2)}) async-start(), calls=%async_computation.5 | async-start | bytes 1310720 | tf_op jit(solution)/shard_map/all_gather | solution.py:1044
  28.0 4.0 %collective-permute-start.4 = (bf16[64,1664]{1,0:T(8,128)(2,1)S(1)}, bf16[64,1664]{1,0:T(8,128)(2,1)S(1)}, u32[]{:S(2)}, u32[]{:S(2)}) collective-permute-start(bf16[64,1664]{1,0:T(8,128)(2,1)S(1)} %collective-permute-done.refs_7_), channel_id=1, source_target_pairs={{0,16},{16,0},{1,17},{17,1},{2,18},{18,2},{3,19},{19,3},{4,20},{20... | collective-permute-start | bytes 638984 | tf_op jit(solution)/shard_map/ppermute | solution.py:803
  28.3 3.7 %collective-permute-start.5 = (bf16[64,1664]{1,0:T(8,128)(2,1)S(1)}, bf16[64,1664]{1,0:T(8,128)(2,1)S(1)}, u32[]{:S(2)}, u32[]{:S(2)}) collective-permute-start(bf16[64,1664]{1,0:T(8,128)(2,1)S(1)} %collective-permute-done.1.refs_8_), channel_id=1, source_target_pairs={{0,16},{16,0},{1,17},{17,1},{2,18},{18,2},{3,19},{19,3},{4,20},{20... | collective-permute-start | bytes 638984 | tf_op jit(solution)/shard_map/ppermute | solution.py:803
  28.6 3.5 %collective-permute-start.6 = (bf16[64,1664]{1,0:T(8,128)(2,1)S(1)}, bf16[64,1664]{1,0:T(8,128)(2,1)S(1)}, u32[]{:S(2)}, u32[]{:S(2)}) collective-permute-start(bf16[64,1664]{1,0:T(8,128)(2,1)S(1)} %collective-permute-done.2.refs_9_), channel_id=1, source_target_pairs={{0,16},{16,0},{1,17},{17,1},{2,18},{18,2},{3,19},{19,3},{4,20},{20... | collective-permute-start | bytes 638984 | tf_op jit(solution)/shard_map/ppermute | solution.py:803
  32.1 26.1 %collective-permute-start.10 = (bf16[528,512]{1,0:T(8,128)(2,1)}, bf16[528,512]{1,0:T(8,128)(2,1)S(1)}, u32[]{:S(2)}, u32[]{:S(2)}) collective-permute-start(bf16[528,512]{1,0:T(8,128)(2,1)} %get-tuple-element.214.refs_9_.refs_8_), channel_id=1, source_target_pairs={{0,1},{1,0},{2,3},{3,2},{4,5},{5,4},{6,7},{7,6},{8,9},{9,8},{10,11... | collective-permute-start | bytes 1622024 | tf_op jit(solution)/shard_map/ppermute | solution.py:766
  33.6 24.6 %collective-permute-start.11 = (bf16[528,512]{1,0:T(8,128)(2,1)}, bf16[528,512]{1,0:T(8,128)(2,1)S(1)}, u32[]{:S(2)}, u32[]{:S(2)}) collective-permute-start(bf16[528,512]{1,0:T(8,128)(2,1)} %get-tuple-element.214.refs_9_.refs_8_), channel_id=1, source_target_pairs={{0,2},{1,3},{2,0},{3,1},{4,6},{5,7},{6,4},{7,5},{8,10},{9,11},{10,... | collective-permute-start | bytes 1622024 | tf_op jit(solution)/shard_map/ppermute | solution.py:766
  35.1 23.1 %collective-permute-start.12 = (bf16[528,512]{1,0:T(8,128)(2,1)}, bf16[528,512]{1,0:T(8,128)(2,1)S(1)}, u32[]{:S(2)}, u32[]{:S(2)}) collective-permute-start(bf16[528,512]{1,0:T(8,128)(2,1)} %get-tuple-element.214.refs_9_.refs_8_), channel_id=1, source_target_pairs={{0,3},{1,2},{2,1},{3,0},{4,7},{5,6},{6,5},{7,4},{8,11},{9,10},{10,... | collective-permute-start | bytes 1622024 | tf_op jit(solution)/shard_map/ppermute | solution.py:766
  35.7 22.6 %copy-start.4 = (bf16[528,512]{1,0:T(8,128)(2,1)S(1)}, bf16[528,512]{1,0:T(8,128)(2,1)}, u32[]{:S(2)}) copy-start(bf16[528,512]{1,0:T(8,128)(2,1)} %get-tuple-element.214.refs_9_.refs_8_) | copy-start | bytes 1622020
  59.4 15.6 %collective-permute-start.13 = (bf16[4,528,512]{2,1,0:T(8,128)(2,1)S(1)}, bf16[4,528,512]{2,1,0:T(8,128)(2,1)S(1)}, u32[]{:S(2)}, u32[]{:S(2)}) collective-permute-start(bf16[4,528,512]{2,1,0:T(8,128)(2,1)S(1)} %pad_maximum_fusion), channel_id=1, source_target_pairs={{0,16},{16,0},{1,17},{17,1},{2,18},{18,2},{3,19},{19,3},{4,20},{20... | collective-permute-start | bytes 6488072 | tf_op jit(solution)/shard_map/ppermute | solution.py:803
  59.4 13.7 %collective-permute-start.7 = (bf16[256,512]{1,0:T(8,128)(2,1)S(1)}, bf16[256,512]{1,0:T(8,128)(2,1)S(1)}, u32[]{:S(2)}, u32[]{:S(2)}) collective-permute-start(bf16[256,512]{1,0:T(8,128)(2,1)S(1)} %copy-done.43), channel_id=1, source_target_pairs={{0,1},{1,0},{2,3},{3,2},{4,5},{5,4},{6,7},{7,6},{8,9},{9,8},{10,11... | collective-permute-start | bytes 786440 | tf_op jit(solution)/shard_map/ppermute | solution.py:766
  60.9 14.0 %collective-permute-start.8 = (bf16[256,512]{1,0:T(8,128)(2,1)S(1)}, bf16[256,512]{1,0:T(8,128)(2,1)S(1)}, u32[]{:S(2)}, u32[]{:S(2)}) collective-permute-start(bf16[256,512]{1,0:T(8,128)(2,1)S(1)} %copy-done.41), channel_id=1, source_target_pairs={{0,2},{1,3},{2,0},{3,1},{4,6},{5,7},{6,4},{7,5},{8,10},{9,11},{10,... | collective-permute-start | bytes 786440 | tf_op jit(solution)/shard_map/ppermute | solution.py:766
  62.4 12.5 %collective-permute-start.9 = (bf16[256,512]{1,0:T(8,128)(2,1)S(1)}, bf16[256,512]{1,0:T(8,128)(2,1)S(1)}, u32[]{:S(2)}, u32[]{:S(2)}) collective-permute-start(bf16[256,512]{1,0:T(8,128)(2,1)S(1)} %copy-done.39), channel_id=1, source_target_pairs={{0,3},{1,2},{2,1},{3,0},{4,7},{5,6},{6,5},{7,4},{8,11},{9,10},{10,... | collective-permute-start | bytes 786440 | tf_op jit(solution)/shard_map/ppermute | solution.py:766
  83.2 133.2 %all-gather.9.cloned.1.call-start = ((), (), s32[]{:S(2)}) async-start(), calls=%async_computation.7 | async-start | bytes 1310720 | tf_op jit(solution)/shard_map/all_gather | solution.py:1045
  92.9 17.3 %copy-start.20 = (bf16[4,16,512]{2,1,0:T(8,128)(2,1)}, bf16[4,16,512]{2,1,0:T(8,128)(2,1)S(1)}, u32[]{:S(2)}) copy-start(bf16[4,16,512]{2,1,0:T(8,128)(2,1)S(1)} %all_to_all.20) | copy-start | bytes 196612
  93.9 16.3 %collective-permute-start.14 = (bf16[256,512]{1,0:T(8,128)(2,1)S(1)}, bf16[256,512]{1,0:T(8,128)(2,1)S(1)}, u32[]{:S(2)}, u32[]{:S(2)}) collective-permute-start(bf16[256,512]{1,0:T(8,128)(2,1)S(1)} %pad_maximum_fusion.2.refs_3_), channel_id=1, source_target_pairs={{0,1},{1,0},{2,3},{3,2},{4,5},{5,4},{6,7},{7,6},{8,9},{9,8},{10,11... | collective-permute-start | bytes 786440 | tf_op jit(solution)/shard_map/ppermute | solution.py:766
  94.8 15.4 %collective-permute-start.15 = (bf16[256,512]{1,0:T(8,128)(2,1)S(1)}, bf16[256,512]{1,0:T(8,128)(2,1)S(1)}, u32[]{:S(2)}, u32[]{:S(2)}) collective-permute-start(bf16[256,512]{1,0:T(8,128)(2,1)S(1)} %pad_maximum_fusion.2.refs_3_), channel_id=1, source_target_pairs={{0,2},{1,3},{2,0},{3,1},{4,6},{5,7},{6,4},{7,5},{8,10},{9,11},{10,... | collective-permute-start | bytes 786440 | tf_op jit(solution)/shard_map/ppermute | solution.py:766
  96.4 13.9 %collective-permute-start.16 = (bf16[256,512]{1,0:T(8,128)(2,1)S(1)}, bf16[256,512]{1,0:T(8,128)(2,1)S(1)}, u32[]{:S(2)}, u32[]{:S(2)}) collective-permute-start(bf16[256,512]{1,0:T(8,128)(2,1)S(1)} %pad_maximum_fusion.2.refs_3_), channel_id=1, source_target_pairs={{0,3},{1,2},{2,1},{3,0},{4,7},{5,6},{6,5},{7,4},{8,11},{9,10},{10,... | collective-permute-start | bytes 786440 | tf_op jit(solution)/shard_map/ppermute | solution.py:766
  142.4 8.1 %collective-permute-start.17 = (bf16[192,576]{1,0:T(8,128)(2,1)}, bf16[192,576]{1,0:T(8,128)(2,1)S(1)}, u32[]{:S(2)}, u32[]{:S(2)}) collective-permute-start(bf16[192,576]{1,0:T(8,128)(2,1)} %get-tuple-element.233), channel_id=1, source_target_pairs={{0,1},{1,0},{2,3},{3,2},{4,5},{5,4},{6,7},{7,6},{8,9},{9,8},{10,11... | collective-permute-start | bytes 663560 | tf_op jit(solution)/shard_map/ppermute | solution.py:766
  143.3 10.4 %collective-permute-start.18 = (bf16[192,576]{1,0:T(8,128)(2,1)}, bf16[192,576]{1,0:T(8,128)(2,1)S(1)}, u32[]{:S(2)}, u32[]{:S(2)}) collective-permute-start(bf16[192,576]{1,0:T(8,128)(2,1)} %get-tuple-element.234), channel_id=1, source_target_pairs={{0,2},{1,3},{2,0},{3,1},{4,6},{5,7},{6,4},{7,5},{8,10},{9,11},{10,... | collective-permute-start | bytes 663560 | tf_op jit(solution)/shard_map/ppermute | solution.py:766
  144.8 8.9 %collective-permute-start.19 = (bf16[192,576]{1,0:T(8,128)(2,1)}, bf16[192,576]{1,0:T(8,128)(2,1)S(1)}, u32[]{:S(2)}, u32[]{:S(2)}) collective-permute-start(bf16[192,576]{1,0:T(8,128)(2,1)} %get-tuple-element.235), channel_id=1, source_target_pairs={{0,3},{1,2},{2,1},{3,0},{4,7},{5,6},{6,5},{7,4},{8,11},{9,10},{10,... | collective-permute-start | bytes 663560 | tf_op jit(solution)/shard_map/ppermute | solution.py:766
  158.5 4.0 %collective-permute-start.20 = (bf16[96,1536]{1,0:T(8,128)(2,1)}, bf16[96,1536]{1,0:T(8,128)(2,1)S(1)}, u32[]{:S(2)}, u32[]{:S(2)}) collective-permute-start(bf16[96,1536]{1,0:T(8,128)(2,1)} %get-tuple-element.241), channel_id=1, source_target_pairs={{0,16},{16,0},{1,17},{17,1},{2,18},{18,2},{3,19},{19,3},{4,20},{20... | collective-permute-start | bytes 884744 | tf_op jit(solution)/shard_map/ppermute | solution.py:803
  158.5 9.7 %all-to-all-start.2 = ((bf16[4,16,512]{2,1,0:T(8,128)(2,1)}), bf16[4,16,512]{2,1,0:T(8,128)(2,1)S(1)}, u32[]{:S(2)}, u32[]{:S(2)}) async-start(bf16[4,16,512]{2,1,0:T(8,128)(2,1)} %bitcast.79), calls=%async_computation.2 | async-start | bytes 131072 | tf_op jit(solution)/shard_map/all_to_all | solution.py:775
  162.5 54.0 %reduce-scatter.4.cloned.1.call-start = ((), (), s32[]{:S(2)}) async-start(), calls=%async_computation.8 | async-start | bytes 368640
  168.3 51.0 %all-gather.7.cloned.1.call-start = ((), (), s32[]{:S(2)}) async-start(), calls=%async_computation.6 | async-start | bytes 1392640 | tf_op jit(solution)/shard_map/all_gather | solution.py:1150
  175.1 13.9 %collective-permute-start.21 = (bf16[256,512]{1,0:T(8,128)(2,1)}, bf16[256,512]{1,0:T(8,128)(2,1)S(1)}, u32[]{:S(2)}, u32[]{:S(2)}) collective-permute-start(bf16[256,512]{1,0:T(8,128)(2,1)} %get-tuple-element.247.refs_14_.refs_23_), channel_id=1, source_target_pairs={{0,1},{1,0},{2,3},{3,2},{4,5},{5,4},{6,7},{7,6},{8,9},{9,8},{10,11... | collective-permute-start | bytes 786440 | tf_op jit(solution)/shard_map/ppermute | solution.py:766
  175.5 13.5 %collective-permute-start.22 = (bf16[256,512]{1,0:T(8,128)(2,1)}, bf16[256,512]{1,0:T(8,128)(2,1)S(1)}, u32[]{:S(2)}, u32[]{:S(2)}) collective-permute-start(bf16[256,512]{1,0:T(8,128)(2,1)} %get-tuple-element.247.refs_14_.refs_23_), channel_id=1, source_target_pairs={{0,2},{1,3},{2,0},{3,1},{4,6},{5,7},{6,4},{7,5},{8,10},{9,11},{10,... | collective-permute-start | bytes 786440 | tf_op jit(solution)/shard_map/ppermute | solution.py:766
  176.4 13.2 %collective-permute-start.23 = (bf16[256,512]{1,0:T(8,128)(2,1)}, bf16[256,512]{1,0:T(8,128)(2,1)S(1)}, u32[]{:S(2)}, u32[]{:S(2)}) collective-permute-start(bf16[256,512]{1,0:T(8,128)(2,1)} %get-tuple-element.247.refs_14_.refs_23_), channel_id=1, source_target_pairs={{0,3},{1,2},{2,1},{3,0},{4,7},{5,6},{6,5},{7,4},{8,11},{9,10},{10,... | collective-permute-start | bytes 786440 | tf_op jit(solution)/shard_map/ppermute | solution.py:766
  216.3 6.4 %collective-permute-start.27 = (bf16[4,64,1792]{2,1,0:T(8,128)(2,1)}, bf16[4,64,1792]{2,1,0:T(8,128)(2,1)S(1)}, u32[]{:S(2)}, u32[]{:S(2)}) collective-permute-start(bf16[4,64,1792]{2,1,0:T(8,128)(2,1)} %get-tuple-element.271), channel_id=1, source_target_pairs={{0,16},{16,0},{1,17},{17,1},{2,18},{18,2},{3,19},{19,3},{4,20},{20... | collective-permute-start | bytes 2752520 | tf_op jit(solution)/shard_map/ppermute | solution.py:803
  219.3 12.4 %collective-permute-start.24 = (bf16[320,512]{1,0:T(8,128)(2,1)}, bf16[320,512]{1,0:T(8,128)(2,1)S(1)}, u32[]{:S(2)}, u32[]{:S(2)}) collective-permute-start(bf16[320,512]{1,0:T(8,128)(2,1)} %get-tuple-element.265), channel_id=1, source_target_pairs={{0,1},{1,0},{2,3},{3,2},{4,5},{5,4},{6,7},{7,6},{8,9},{9,8},{10,11... | collective-permute-start | bytes 983048 | tf_op jit(solution)/shard_map/ppermute | solution.py:766
  220.7 16.4 %collective-permute-start.25 = (bf16[320,512]{1,0:T(8,128)(2,1)}, bf16[320,512]{1,0:T(8,128)(2,1)S(1)}, u32[]{:S(2)}, u32[]{:S(2)}) collective-permute-start(bf16[320,512]{1,0:T(8,128)(2,1)} %get-tuple-element.266), channel_id=1, source_target_pairs={{0,2},{1,3},{2,0},{3,1},{4,6},{5,7},{6,4},{7,5},{8,10},{9,11},{10,... | collective-permute-start | bytes 983048 | tf_op jit(solution)/shard_map/ppermute | solution.py:766
  221.3 15.8 %collective-permute-start.26 = (bf16[320,512]{1,0:T(8,128)(2,1)}, bf16[320,512]{1,0:T(8,128)(2,1)S(1)}, u32[]{:S(2)}, u32[]{:S(2)}) collective-permute-start(bf16[320,512]{1,0:T(8,128)(2,1)} %get-tuple-element.267), channel_id=1, source_target_pairs={{0,3},{1,2},{2,1},{3,0},{4,7},{5,6},{6,5},{7,4},{8,11},{9,10},{10,... | collective-permute-start | bytes 983048 | tf_op jit(solution)/shard_map/ppermute | solution.py:766
  224.6 12.6 %copy-start.23 = (bf16[320,512]{1,0:T(8,128)(2,1)S(1)}, bf16[320,512]{1,0:T(8,128)(2,1)}, u32[]{:S(2)}) copy-start(bf16[320,512]{1,0:T(8,128)(2,1)} %get-tuple-element.277) | copy-start | bytes 983044
  237.1 13.6 %copy-start.22 = (f32[256,512]{1,0:T(8,128)S(1)}, f32[256,512]{1,0:T(8,128)}, u32[]{:S(2)}) copy-start(f32[256,512]{1,0:T(8,128)} %get-tuple-element.286) | copy-start | bytes 1572868
  237.1 13.6 %copy-start.24 = (bf16[64,256]{1,0:T(8,128)(2,1)S(1)}, bf16[64,256]{1,0:T(8,128)(2,1)}, u32[]{:S(2)}) copy-start(bf16[64,256]{1,0:T(8,128)(2,1)} %get-tuple-element.212.refs_7_.refs_2_) | copy-start | bytes 98308
  237.1 2.2 collective-permute-start.28
  240.3 10.3 %all-to-all-start.3 = ((bf16[4,16,512]{2,1,0:T(8,128)(2,1)}), bf16[4,16,512]{2,1,0:T(8,128)(2,1)S(1)}, u32[]{:S(2)}, u32[]{:S(2)}) async-start(bf16[4,16,512]{2,1,0:T(8,128)(2,1)} %bitcast.24), calls=%async_computation.3 | async-start | bytes 131072 | tf_op jit(solution)/shard_map/all_to_all | solution.py:775
  244.9 50.1 %all-reduce.4.cloned.1.call-start = ((), (), s32[]{:S(2)}) async-start(), calls=%async_computation.9 | async-start | bytes 1261568 | tf_op jit(solution)/shard_map/psum | solution.py:1259
  244.9 8.5 %collective-permute-start.29 = (bf16[64,1792]{1,0:T(8,128)(2,1)S(1)}, bf16[64,1792]{1,0:T(8,128)(2,1)S(1)}, u32[]{:S(2)}, u32[]{:S(2)}) collective-permute-start(bf16[64,1792]{1,0:T(8,128)(2,1)S(1)} %get-tuple-element.289), channel_id=1, source_target_pairs={{0,1},{1,0},{2,3},{3,2},{4,5},{5,4},{6,7},{7,6},{8,9},{9,8},{10,11... | collective-permute-start | bytes 688136 | tf_op jit(solution)/shard_map/ppermute | solution.py:766
  245.5 12.0 %collective-permute-start.30 = (bf16[64,1792]{1,0:T(8,128)(2,1)S(1)}, bf16[64,1792]{1,0:T(8,128)(2,1)S(1)}, u32[]{:S(2)}, u32[]{:S(2)}) collective-permute-start(bf16[64,1792]{1,0:T(8,128)(2,1)S(1)} %get-tuple-element.290), channel_id=1, source_target_pairs={{0,2},{1,3},{2,0},{3,1},{4,6},{5,7},{6,4},{7,5},{8,10},{9,11},{10,... | collective-permute-start | bytes 688136 | tf_op jit(solution)/shard_map/ppermute | solution.py:766
  247.0 10.6 %collective-permute-start.31 = (bf16[64,1792]{1,0:T(8,128)(2,1)S(1)}, bf16[64,1792]{1,0:T(8,128)(2,1)S(1)}, u32[]{:S(2)}, u32[]{:S(2)}) collective-permute-start(bf16[64,1792]{1,0:T(8,128)(2,1)S(1)} %get-tuple-element.291), channel_id=1, source_target_pairs={{0,3},{1,2},{2,1},{3,0},{4,7},{5,6},{6,5},{7,4},{8,11},{9,10},{10,... | collective-permute-start | bytes 688136 | tf_op jit(solution)/shard_map/ppermute | solution.py:766
  250.9 28.2 %copy-start.19 = (bf16[256,512]{1,0:T(8,128)(2,1)}, bf16[256,512]{1,0:T(8,128)(2,1)S(1)}, u32[]{:S(2)}) copy-start(bf16[256,512]{1,0:T(8,128)(2,1)S(1)} %fusion.refs_0_) | copy-start | bytes 786436
  257.6 7.3 %collective-permute-start.34 = (bf16[16,1792]{1,0:T(8,128)(2,1)S(1)}, bf16[16,1792]{1,0:T(8,128)(2,1)S(1)}, u32[]{:S(2)}, u32[]{:S(2)}) collective-permute-start(bf16[16,1792]{1,0:T(8,128)(2,1)S(1)} %get-tuple-element.342), channel_id=1, source_target_pairs={{0,12},{4,0},{8,4},{12,8},{1,13},{5,1},{9,5},{13,9},{2,14},{6,2},{... | collective-permute-start | bytes 172040 | tf_op jit(solution)/shard_map/ppermute | solution.py:786
  261.2 10.9 %collective-permute-start.33 = (bf16[16,1792]{1,0:T(8,128)(2,1)S(1)}, bf16[16,1792]{1,0:T(8,128)(2,1)S(1)}, u32[]{:S(2)}, u32[]{:S(2)}) collective-permute-start(bf16[16,1792]{1,0:T(8,128)(2,1)S(1)} %get-tuple-element.343), channel_id=1, source_target_pairs={{0,8},{4,12},{8,0},{12,4},{1,9},{5,13},{9,1},{13,5},{2,10},{6,14},... | collective-permute-start | bytes 172040 | tf_op jit(solution)/shard_map/ppermute | solution.py:786
  261.2 10.9 %collective-permute-start.32 = (bf16[16,1792]{1,0:T(8,128)(2,1)S(1)}, bf16[16,1792]{1,0:T(8,128)(2,1)S(1)}, u32[]{:S(2)}, u32[]{:S(2)}) collective-permute-start(bf16[16,1792]{1,0:T(8,128)(2,1)S(1)} %get-tuple-element.341), channel_id=1, source_target_pairs={{0,4},{4,8},{8,12},{12,0},{1,5},{5,9},{9,13},{13,1},{2,6},{6,10},{... | collective-permute-start | bytes 172040 | tf_op jit(solution)/shard_map/ppermute | solution.py:786
  262.4 9.8 %collective-permute-start.35 = (bf16[256,512]{1,0:T(8,128)(2,1)S(1)}, bf16[256,512]{1,0:T(8,128)(2,1)S(1)}, u32[]{:S(2)}, u32[]{:S(2)}) collective-permute-start(bf16[256,512]{1,0:T(8,128)(2,1)S(1)} %fusion.refs_0_), channel_id=1, source_target_pairs={{0,1},{1,0},{2,3},{3,2},{4,5},{5,4},{6,7},{7,6},{8,9},{9,8},{10,11... | collective-permute-start | bytes 786440 | tf_op jit(solution)/shard_map/ppermute | solution.py:766
  263.8 11.2 %collective-permute-start.36 = (bf16[256,512]{1,0:T(8,128)(2,1)S(1)}, bf16[256,512]{1,0:T(8,128)(2,1)S(1)}, u32[]{:S(2)}, u32[]{:S(2)}) collective-permute-start(bf16[256,512]{1,0:T(8,128)(2,1)S(1)} %fusion.refs_0_), channel_id=1, source_target_pairs={{0,2},{1,3},{2,0},{3,1},{4,6},{5,7},{6,4},{7,5},{8,10},{9,11},{10,... | collective-permute-start | bytes 786440 | tf_op jit(solution)/shard_map/ppermute | solution.py:766
  265.0 10.1 %collective-permute-start.37 = (bf16[256,512]{1,0:T(8,128)(2,1)S(1)}, bf16[256,512]{1,0:T(8,128)(2,1)S(1)}, u32[]{:S(2)}, u32[]{:S(2)}) collective-permute-start(bf16[256,512]{1,0:T(8,128)(2,1)S(1)} %fusion.refs_0_), channel_id=1, source_target_pairs={{0,3},{1,2},{2,1},{3,0},{4,7},{5,6},{6,5},{7,4},{8,11},{9,10},{10,... | collective-permute-start | bytes 786440 | tf_op jit(solution)/shard_map/ppermute | solution.py:766
  275.1 7.5 %collective-permute-start.38 = (bf16[16,1792]{1,0:T(8,128)(2,1)S(1)}, bf16[16,1792]{1,0:T(8,128)(2,1)S(1)}, u32[]{:S(2)}, u32[]{:S(2)}) collective-permute-start(bf16[16,1792]{1,0:T(8,128)(2,1)S(1)} %add_convert_fusion.2), channel_id=1, source_target_pairs={{0,12},{4,0},{8,4},{12,8},{1,13},{5,1},{9,5},{13,9},{2,14},{6,2},{... | collective-permute-start | bytes 172040 | tf_op jit(solution)/shard_map/ppermute | solution.py:793
  278.0 5.2 %collective-permute-start.39 = (bf16[16,1792]{1,0:T(8,128)(2,1)S(1)}, bf16[16,1792]{1,0:T(8,128)(2,1)S(1)}, u32[]{:S(2)}, u32[]{:S(2)}) collective-permute-start(bf16[16,1792]{1,0:T(8,128)(2,1)S(1)} %add_convert_fusion.2), channel_id=1, source_target_pairs={{0,8},{4,12},{8,0},{12,4},{1,9},{5,13},{9,1},{13,5},{2,10},{6,14},... | collective-permute-start | bytes 172040 | tf_op jit(solution)/shard_map/ppermute | solution.py:793
  278.8 7.2 %collective-permute-start.40 = (bf16[16,1792]{1,0:T(8,128)(2,1)S(1)}, bf16[16,1792]{1,0:T(8,128)(2,1)S(1)}, u32[]{:S(2)}, u32[]{:S(2)}) collective-permute-start(bf16[16,1792]{1,0:T(8,128)(2,1)S(1)} %add_convert_fusion.2), channel_id=1, source_target_pairs={{0,4},{4,8},{8,12},{12,0},{1,5},{5,9},{9,13},{13,1},{2,6},{6,10},{... | collective-permute-start | bytes 172040 | tf_op jit(solution)/shard_map/ppermute | solution.py:793
  282.6 24.2 %copy-start.2 = (s32[6]{0:T(128)S(1)}, s32[6]{0:T(128)}, u32[]{:S(2)}) copy-start(s32[6]{0:T(128)} %stack.57.perm_ref) | copy-start | bytes 76
  295.1 14.1 %copy-start.18 = (bf16[1024,512]{1,0:T(8,128)(2,1)S(1)}, bf16[1024,512]{1,0:T(8,128)(2,1)}, u32[]{:S(2)}) copy-start(bf16[1024,512]{1,0:T(8,128)(2,1)} %all-gather.9.cloned.1.call-done) | copy-start | bytes 3145732
  295.1 5.2 %collective-permute-start.41 = (bf16[544,512]{1,0:T(8,128)(2,1)}, bf16[544,512]{1,0:T(8,128)(2,1)S(1)}, u32[]{:S(2)}, u32[]{:S(2)}) collective-permute-start(bf16[544,512]{1,0:T(8,128)(2,1)} %get-tuple-element.308.mine_ref), channel_id=1, source_target_pairs={{0,16},{16,0},{1,17},{17,1},{2,18},{18,2},{3,19},{19,3},{4,20},{20... | collective-permute-start | bytes 1671176 | tf_op jit(solution)/shard_map/ppermute | solution.py:803
  295.4 9.6 %collective-permute-start.45 = (bf16[64,1792]{1,0:T(8,128)(2,1)S(1)}, bf16[64,1792]{1,0:T(8,128)(2,1)S(1)}, u32[]{:S(2)}, u32[]{:S(2)}) collective-permute-start(bf16[64,1792]{1,0:T(8,128)(2,1)S(1)} %constant_dynamic-slice_fusion.mine_ref), channel_id=1, source_target_pairs={{0,16},{16,0},{1,17},{17,1},{2,18},{18,2},{3,19},{19,3},{4,20},{20... | collective-permute-start | bytes 688136 | tf_op jit(solution)/shard_map/ppermute | solution.py:803
  296.8 7.9 %collective-permute-start.42 = (bf16[32,1536]{1,0:T(8,128)(2,1)S(1)}, bf16[32,1536]{1,0:T(8,128)(2,1)S(1)}, u32[]{:S(2)}, u32[]{:S(2)}) collective-permute-start(bf16[32,1536]{1,0:T(8,128)(2,1)S(1)} %constant_dynamic-update-slice_fusion.8), channel_id=1, source_target_pairs={{0,1},{1,0},{2,3},{3,2},{4,5},{5,4},{6,7},{7,6},{8,9},{9,8},{10,11... | collective-permute-start | bytes 294920 | tf_op jit(solution)/shard_map/ppermute | solution.py:766
  298.1 6.6 %collective-permute-start.43 = (bf16[32,1536]{1,0:T(8,128)(2,1)S(1)}, bf16[32,1536]{1,0:T(8,128)(2,1)S(1)}, u32[]{:S(2)}, u32[]{:S(2)}) collective-permute-start(bf16[32,1536]{1,0:T(8,128)(2,1)S(1)} %constant_dynamic-update-slice_fusion.8), channel_id=1, source_target_pairs={{0,2},{1,3},{2,0},{3,1},{4,6},{5,7},{6,4},{7,5},{8,10},{9,11},{10,... | collective-permute-start | bytes 294920 | tf_op jit(solution)/shard_map/ppermute | solution.py:766
  299.4 5.5 %collective-permute-start.44 = (bf16[32,1536]{1,0:T(8,128)(2,1)S(1)}, bf16[32,1536]{1,0:T(8,128)(2,1)S(1)}, u32[]{:S(2)}, u32[]{:S(2)}) collective-permute-start(bf16[32,1536]{1,0:T(8,128)(2,1)S(1)} %constant_dynamic-update-slice_fusion.8), channel_id=1, source_target_pairs={{0,3},{1,2},{2,1},{3,0},{4,7},{5,6},{6,5},{7,4},{8,11},{9,10},{10,... | collective-permute-start | bytes 294920 | tf_op jit(solution)/shard_map/ppermute | solution.py:766
  305.0 1.8 collective-permute-start.46
  (36 other events, 110.6 us)
Sparse Core Ops, SparseCore 0:
  83.3 30.6 all-gather.4
  115.8 25.7 all-gather.8
  168.4 22.7 reduce-scatter.3
  192.9 26.3 all-gather.6
  248.6 46.3 all-reduce.3
where the time goes:
time: 318 us; the launch traced here: 317 us
  Pallas kernels  154 us (48%)
  starting transfers between devices  60.5 us (19%)
  waiting for transfers between devices  58.7 us (18%)
  between operations  14.5 us (5%)
  local copies, waits for them, and re-layouts  11.6 us (4%)
  blocking collectives  9.65 us (3%)
  other arithmetic  7.56 us (2%)
    pallas_call x15, Pallas kernels, call(): pl.pallas_call(body, grid_spec=spec, out_shape=[(pltpu.HBM if name in PIN...  154 us
    ppermute x30, starting transfers between devices, across(): return lax.ppermute(value, 'mp', pairs)  36.1 us
    ppermute x30, waiting for transfers between devices, across(): return lax.ppermute(value, 'mp', pairs)  25.3 us
    all_to_all x3, starting transfers between devices, exchange(): return lax.all_to_all(value, 'res', split_axis=0, concat_axis=0, tiled=True)  13.9 us
    all_to_all x1, blocking collectives, exchange(): return lax.all_to_all(value, 'res', split_axis=0, concat_axis=0, tiled=True)  9.65 us
    psum x1, waiting for transfers between devices, per_device(): early, whole = lax.psum((early, whole), 'res')  9.01 us
    all_to_all x3, waiting for transfers between devices, exchange(): return lax.all_to_all(value, 'res', split_axis=0, concat_axis=0, tiled=True)  8.64 us
    unnamed x99, local copies, waits for them, and re-layouts  8.03 us
  transfers between devices with their start and end apart: 55, of which 20 were waited for; matrix products, arithmetic and copies ran while one was open for 3% of the time, Pallas kernels for 45%

commit v1 on v0

--- a/solution.py
+++ b/solution.py
@@ -72,6 +72,11 @@
     return inverse * inner
 
 
+def chosen_row(value, row):
+    rows = lax.broadcasted_iota(jnp.int32, value.shape, 0)
+    return jnp.sum(jnp.where(rows == row, value.astype(F32), 0.0), axis=0, keepdims=True)
+
+
 def selector(slot_row, rows):
     positions = lax.broadcasted_iota(jnp.int16, (rows, slot_row.shape[1]), 0)
     return jnp.where(positions == slot_row.astype(jnp.int16), low(1.0), low(0.0))
@@ -87,8 +92,8 @@
     return jnp.concatenate([fixed, term], axis=1)
 
 
-def message_forward_body(perm_ref, *refs, count, calls):
-    edge_ref, slot_ref, node_ref, arrive_ref, fixed_ref, scale_ref = refs[:6]
+def message_forward_body(perm_ref, *refs, count, calls, start):
+    edge_ref, slot_ref, node_ref, arrive_ref, fixed_ref, count_ref = refs[:6]
     weights = refs[6 : 6 + count]
     others = refs[6 + count : 6 + 2 * count]
     refs = refs[6 + 2 * count :]
@@ -131,7 +136,8 @@
         return carry
 
     lax.fori_loop(0, steps // group, some, 0)
-    mean = (sum_ref[...] * scale_ref[0]).astype(BF16)
+    scale = 1.0 / jnp.maximum(chosen_row(count_ref[...], perm_ref[number + start]), 1.0)
+    mean = (sum_ref[...] * scale).astype(BF16)
     mean_ref[0] = mean
     total = dot_tn(mean, weight_ref[:, 2 * width : 3 * width]).astype(BF16)
     for spot in range(calls):
@@ -139,6 +145,16 @@
         @pl.when(number == spot)
         def _(spot=spot):
             parts[spot][...] = total
+
+
+def send_selector(rows, lanes):
+    peers, slots = rows.shape
+    lane = lax.broadcasted_iota(jnp.int32, (slots, lanes), 1).astype(F32)
+    parts = []
+    for peer in range(peers):
+        column = jnp.broadcast_to(rows[peer : peer + 1, :].astype(F32), (8, slots)).T[:, 0:1]
+        parts.append(jnp.where(lane == column, 1.0, 0.0).astype(BF16))
+    return jnp.concatenate(parts, axis=0)
 
 
 def pack_body(perm_ref, nodes_ref, output_ref, bias_ref, send_ref, node_ref, pack_ref, leave_ref, all_ref, *, count):
@@ -155,9 +171,7 @@
     pack_ref[...] = all_ref[pl.ds(start, half), :]
     proteins, lanes, _ = node_ref.shape
     for spot in range(proteins):
-        rows = tall(send_ref[spot : spot + 1, :].astype(F32))
-        lane = lax.broadcasted_iota(jnp.int32, (rows.shape[0], lanes), 1).astype(F32)
-        table = jnp.where(lane == rows, 1.0, 0.0).astype(BF16)
+        table = send_selector(send_ref[spot, 0], lanes)
         leave_ref[:, spot] = dot(table, node_ref[spot]).astype(BF16).reshape(leave_ref[:, spot].shape)
 
 
@@ -230,15 +244,10 @@
     vector_ref[4:6, :] = shifts_ref[...].astype(F32)
     vector_ref[6:8, :] = jnp.zeros((2, vector_ref.shape[1]), F32)
     me = perm_ref[0]
-    pick = lambda value: jnp.sum(
-        jnp.where(lax.broadcasted_iota(jnp.int32, value.shape, 0) == me, value, 0.0), axis=0, keepdims=True
-    )
-    counts = pick(counts_ref[...].astype(F32))
+    counts = chosen_row(counts_ref[...], me)
     share = counts * (1.0 / jnp.maximum(counts, 1.0))
     share_ref[...] = jnp.broadcast_to(tall(share), share_ref.shape)
-    rows = tall(pick(send_ref[...].astype(F32)))
-    lane = lax.broadcasted_iota(jnp.int32, table_ref.shape, 1).astype(F32)
-    table_ref[...] = jnp.where(lane == rows, 1.0, 0.0).astype(BF16)
+    table_ref[...] = send_selector(send_ref[me, 0], table_ref.shape[1])
     wide_bias_ref[...] = jnp.broadcast_to(wide, wide_bias_ref.shape).astype(BF16)
     own_node_ref[...] = node_ref[...]
     own_up_ref[...] = up_ref[...]
@@ -406,8 +415,8 @@
 
 def return_body(perm_ref, *refs, count):
     sums = refs[:count]
-    turned_ref, up_ref, low_ref, arrive_ref, grad_ref, column_ref = refs[count : count + 6]
-    second_ref, leave_ref, mine_ref, other_ref, whole_ref = refs[count + 6 :]
+    turned_ref, up_ref = refs[count : count + 2]
+    second_ref, leave_ref, sum_ref = refs[count + 2 :]
     total = sums[0][...].astype(F32)
     for spot in range(1, count):
         total = total + sums[spot][...].astype(F32)
@@ -418,6 +427,13 @@
     second_ref[...] = (
         up_ref[0].astype(F32) + dot_tn(low[:, 0:lanes], turned_ref[:, 0:width]) + back[0:lanes]
     )
+    sum_ref[...] = total
+
+
+def update_weights_body(perm_ref, sum_ref, low_ref, arrive_ref, grad_ref, column_ref, whole_ref):
+    total = sum_ref[...]
+    low = total.astype(BF16)
+    lanes = low_ref.shape[0]
     channels = grad_ref.shape[0]
     hidden = low.shape[0]
     rows = jnp.concatenate([low_ref[...], arrive_ref[...]], axis=0)
@@ -441,10 +457,6 @@
         ],
         axis=1,
     )
-    core = perm_ref[count + 1]
-    half = mine_ref.shape[0]
-    mine_ref[...] = whole_ref[pl.ds(pl.multiple_of(core * half, 8), half), :]
-    other_ref[...] = whole_ref[pl.ds(pl.multiple_of((1 - core) * half, 8), half), :].astype(BF16)
 
 
 def backward_body(*refs, count):
@@ -486,15 +498,15 @@
 
 
 def message_backward_body(perm_ref, *refs, count, calls, first_call):
-    edge_ref, slot_ref, slope_ref, part_ref, edge_weight_ref, scale_ref = refs[:6]
+    edge_ref, slot_ref, slope_ref, part_ref, edge_weight_ref, count_ref = refs[:6]
     weights = refs[6 : 6 + count]
     others = refs[6 + count : 6 + 2 * count]
     ups = refs[6 + 2 * count : 6 + 2 * count + calls]
     refs = refs[6 + 2 * count + calls :]
     if not first_call:
         node_ref, arrive_ref, own_node_ref, own_arrive_ref, mean_ref, own_mean_ref = refs[:6]
-        own_up_ref, own_low_ref, own_edge_ref = refs[6:9]
-        refs = refs[10:]
+        own_up_ref, own_low_ref, own_edge_ref, whole_ref = refs[6:10]
+        refs = refs[11:]
     grad_ref = refs[0]
     backs = refs[1 : 1 + calls]
     low_out_ref, edge_out_ref = refs[1 + calls : 3 + calls]
@@ -528,7 +540,9 @@
         @pl.when(number == spot)
         def _(spot=spot):
             value = dot_nt(weight_ref[:, 2 * width : 3 * width], ups[spot][...])
-            up_ref[...] = (value * scale_ref[0]).astype(BF16)
+            number_of = perm_ref[spot if first_call else spot + 1]
+            scale = 1.0 / jnp.maximum(chosen_row(count_ref[...], number_of), 1.0)
+            up_ref[...] = (value * scale).astype(BF16)
             if not first_call:
                 at = (spot + 1) * pool
                 row_ref[at : at + lanes, :] = node_ref[0]
@@ -593,13 +607,25 @@
         bias_ref[...] = dot(low_ref[0:hidden, :], ones)
         core = perm_ref[count + 1]
         half = part // 2
+        rows = whole_ref.shape[0] // count // 2
         for spot in range(count):
             for place, ref in ((core, mine_ref), (1 - core, other_ref)):
                 first = pl.multiple_of(spot * part + place * half, half)
                 kind = ref.dtype
-                ref[spot, :, 0:width] = total_ref[pl.ds(first, half), :].astype(kind)
-                ref[spot, :, width : 2 * width] = total_ref[pl.ds(hidden + first, half), :].astype(kind)
-                ref[spot, :, 2 * width : 3 * width] = out_total_ref[pl.ds(first, half), :].astype(kind)
+                ref[spot, 0:half, 0:width] = total_ref[pl.ds(first, half), :].astype(kind)
+                ref[spot, 0:half, width : 2 * width] = total_ref[pl.ds(hidden + first, half), :].astype(kind)
+                ref[spot, 0:half, 2 * width : 3 * width] = out_total_ref[pl.ds(first, half), :].astype(kind)
+                start = pl.multiple_of((place * count + perm_ref[spot]) * rows, 8)
+                wide = whole_ref.shape[1]
+                below = jnp.concatenate(
+                    [
+                        whole_ref[pl.ds(start, rows), :],
+                        jnp.zeros((ref.shape[1] - half - rows, wide), F32),
+                    ],
+                    axis=0,
+                )
+                ref[spot, half:, 0:wide] = below.astype(kind)
+                ref[spot, half:, wide:] = jnp.zeros((below.shape[0], ref.shape[2] - wide), kind)
                 both = jnp.concatenate(
                     [
                         edge_total_ref[pl.ds(first, half), :],
@@ -607,7 +633,7 @@
                     ],
                     axis=1,
                 )
-                ref[spot, :, 3 * width :] = both.astype(kind)
+                ref[spot, 0:half, 3 * width :] = both.astype(kind)
 
 
 def wide_body(
@@ -626,10 +652,10 @@
         line = forward_ref[spot * step + lanes : (spot + 1) * step, :].astype(F32)
         lines = line if spot == 0 else lines + line
     pre = dot(low, weight_ref[...]) + bias_ref[0:1, :].astype(F32)
-    out, slope = gelu_pair(pre)
-    grad = slope * dot_nt(forward, output_ref[...])
+    out, slope = gelu_pair_low(pre)
+    grad = slope.astype(F32) * dot_nt(forward, output_ref[...])
     all_ref[0:width, :] = dot_tn(low, grad.astype(BF16))
-    all_ref[width : width + wide, :] = dot_tn(out.astype(BF16), forward)
+    all_ref[width : width + wide, :] = dot_tn(out, forward)
     at = width + wide
     total = jnp.broadcast_to(jnp.sum(grad, axis=0, keepdims=True), (8, wide))
     all_ref[at : at + 8, :] = total
@@ -722,8 +748,12 @@
             refs[count][0] = refs[spot][...]
 
 
+def held(value):
+    return pltpu.with_memory_space_constraint(value, pltpu.HBM)
+
+
 def group_of(total):
-    for size in (5, 4, 3, 2, 1):
+    for size in (15, 5, 4, 3, 2, 1):
         if total % size == 0:
             return size
 
@@ -850,7 +880,6 @@
                 [lax.dynamic_slice_in_dim(value, spot * size, size, axis) for spot in order], axis=axis
             )
 
-        send_flat = send_rows.reshape(proteins, -1)
         message_pack, leaving = call(
             functools.partial(pack_body, count=mp_size),
             (1,),
@@ -858,7 +887,7 @@
                 (message_nodes,),
                 (message_output,),
                 (message_bias,),
-                (send_flat,),
+                (send_rows,),
                 (node_states,),
             ],
             [
@@ -877,8 +906,6 @@
         own_slots = lax.dynamic_slice_in_dim(neighbour_slots, me * own_k, own_k, 2)
         alive = lax.broadcasted_iota(jnp.int32, own_slots.shape, 2) + me * own_k < live_counts[..., None]
         own_slots = jnp.transpose(jnp.where(alive, own_slots, dead), (0, 2, 1))
-        counts = live_counts.astype(F32)
-        scale = (1.0 / jnp.maximum(counts, 1.0))[:, None, :]
         edges = jnp.transpose(edge_states, (0, 2, 3, 1))
         edge_up = jnp.transpose(edge_cotangent, (0, 2, 3, 1))
         turned = update_weight.T
@@ -898,7 +925,7 @@
                 (norm_gains,),
                 (norm_shifts,),
                 (live_counts,),
-                (send_flat,),
+                (send_rows,),
                 (node_states, (1, lanes, width), lambda p, perm: (perm[0], 0, 0)),
                 (node_cotangent, (1, lanes, width), lambda p, perm: (perm[0], 0, 0)),
                 (feedforward_weight,),
@@ -924,8 +951,8 @@
             "prepare",
             perm,
         )
-        weights, other_weights, arriving, own_slots, scale, small = lax.optimization_barrier(
-            (weights, other_weights, arriving, own_slots, scale, small)
+        weights, other_weights, arriving, own_slots, small = lax.optimization_barrier(
+            (weights, other_weights, arriving, own_slots, small)
         )
         (
             edge_weight,
@@ -973,17 +1000,14 @@
                 (arriving, (res_size, 1, slots, width), by_arrive),
             ]
 
-        def scale_in(start):
-            return (scale, (1, 1, lanes), shifted(start)[1])
-
         def message_forward(start, calls, after):
             slots_after, _ = lax.optimization_barrier((own_slots, after))
             found = call(
-                functools.partial(message_forward_body, count=proteins, calls=calls),
+                functools.partial(message_forward_body, count=proteins, calls=calls, start=start),
                 (calls,),
                 [edge_ins(start)[0], (slots_after,) + edge_ins(start)[1][1:]]
                 + row_ins(start)
-                + [(edge_weight_t,), scale_in(start)]
+                + [(edge_weight_t,), (live_counts,)]
                 + [(value,) for value in weights + other_weights],
                 [
                     ((calls, own_k, hidden, lanes), BF16, slope_block, by_step4),
@@ -1015,8 +1039,8 @@
             (),
             [(value,) for value in parts]
             + [(own_node,), (share,), (vectors,), (own_table,), (turned,)]
-            + [(value,) for value in blocks]
-            + [(other_blocks,)],
+            + [(held(value),) for value in blocks]
+            + [(held(other_blocks),)],
             [
                 ((lanes, width), F32),
                 ((lanes, width), F32),
@@ -1030,7 +1054,7 @@
             4 * lanes * width * wide * mp_size,
             4 * width * wide * mp_size,
             "feed_forward",
-            limit=56,
+            limit=24,
         )
 
         arrived = exchange(leaving.reshape(res_size, slots, width)).reshape(remote, width)
@@ -1106,34 +1130,41 @@
         sums_own, sums_others, all_low = lax.optimization_barrier((sums_own, sums_others, all_low))
         sums = scatter(list(sums_own) + list(sums_others))
         whole_width = turned_width + update_hidden + 128
-        second_part, leaving, whole_mine, whole_other = call(
+        second_part, leaving, update_sums = call(
             functools.partial(return_body, count=proteins),
             (1,),
             [(value,) for value in sums]
-            + [(turned,), (own_up,), (second_low,), (arrived,), (grads,), (columns,)],
+            + [(turned,), (own_up,)],
             [
                 ((lanes, width), F32),
                 ((remote, width), BF16),
-                ((update_hidden // 2, whole_width), F32),
-                ((update_hidden // 2, whole_width), BF16),
+                ((update_hidden, lanes + pool), F32),
             ],
-            [pltpu.VMEM((update_hidden, whole_width), F32)],
+            [],
             2 * (lanes + pool) * width * update_hidden,
             (lanes + pool) * width * 2,
             "update_return",
             perm,
         )
-        whole_swapped = swap(whole_other)
         returned = exchange(leaving.reshape(res_size, slots, width)).reshape(remote, width)
-        whole = (whole_mine + whole_swapped.astype(F32)).astype(BF16)
+        (whole,) = call(
+            update_weights_body,
+            (1,),
+            [(update_sums,), (second_low,), (arrived,), (grads,), (columns,)],
+            [((update_hidden, whole_width), F32)],
+            [],
+            2 * (lanes + pool) * width * update_hidden,
+            (lanes + pool) * width * 2,
+            "update_weights",
+            perm,
+        )
         whole, returned = lax.optimization_barrier((whole, returned))
-        whole = lax.psum_scatter(whole, "mp", scatter_dimension=0, tiled=True)
         aggregate_grad, forward_grad, sum_one, _ = call(
             functools.partial(backward_body, count=proteins),
             (),
             [(second_part,), (returned,), (own_table,), (one,), (two,), (share,), (vectors,), (wide_slope,)]
-            + [(value,) for value in blocks]
-            + [(other_blocks,)],
+            + [(held(value),) for value in blocks]
+            + [(held(other_blocks),)],
             [
                 ((lanes, width), BF16),
                 ((lanes + 16, width), BF16),
@@ -1144,12 +1175,14 @@
             6 * lanes * width * wide * mp_size,
             4 * width * wide * mp_size,
             "feed_backward",
-            limit=56,
+            limit=24,
         )
         ups = gather(aggregate_grad)
         all_forward = lax.all_gather(forward_grad, "mp", axis=0, tiled=True)
         total_width = 3 * width + -(-(channels + 1) // 128) * 128
-        late_shape = (proteins, part // 2, total_width)
+        whole_rows = update_hidden // 2 // mp_size
+        late_rows = -(-(part // 2 + whole_rows) // (8 * res_size)) * 8 * res_size
+        late_shape = (proteins, late_rows, total_width)
 
         def message_backward(start, calls, earlier):
             by_perm4 = shifted(start)[0]
@@ -1159,7 +1192,7 @@
                     (slope_own if earlier is None else slope_others, slope_block, by_step4),
                     (edge_part_own if earlier is None else edge_part_others, edge_block, by_step4),
                     (edge_weight,),
-                    scale_in(start),
+                    (live_counts,),
                 ]
                 + [(value,) for value in weights + other_weights + ups[start : start + calls]]
             )
@@ -1185,6 +1218,7 @@
                     (ups[0],),
                     (earlier[1],),
                     (earlier[2],),
+                    (whole,),
                     (earlier[0], None),
                 ]
                 aliases = ((len(ins) - 1, 0),)
@@ -1221,8 +1255,8 @@
         )
         found = list(back_own) + list(back_others)
         late_swapped = swap(late_other)
-        backs, late_mine, all_forward, node_result, whole = lax.optimization_barrier(
-            (found, late_mine, all_forward, node_result, whole)
+        backs, late_mine, all_forward, node_result = lax.optimization_barrier(
+            (found, late_mine, all_forward, node_result)
         )
         back = scatter(backs)
         late = late_mine + late_swapped.astype(F32)
@@ -1256,7 +1290,8 @@
         leaving, early_swapped = lax.optimization_barrier((leaving, early_swapped))
         early = (early_mine + early_swapped.astype(F32)).astype(BF16)
         early, leaving = lax.optimization_barrier((early, leaving))
-        early, whole = lax.psum((early, whole), "res")
+        cut = early.shape[0] // 2
+        early = jnp.concatenate(lax.psum((early[:cut], early[cut:]), "res"), axis=0)
         returned = exchange(leaving)
         node_grad = (
             sum_one
@@ -1279,14 +1314,14 @@
             [((proteins, lanes, width), BF16, (1, lanes, width), shifted(0)[1])],
             [],
             0,
-            4 * proteins * lanes * width,
+            0,
             "place_rows",
             perm,
         )
-        early, whole, node_grad, late_parts = lax.optimization_barrier(
-            (early, whole, node_grad, late_parts)
-        )
+        early, node_grad, late_parts = lax.optimization_barrier((early, node_grad, late_parts))
         late = block_order(late_parts)
+        whole = late[part // 2 : part // 2 + whole_rows, :whole_width]
+        late = late[: part // 2]
         early_swapped = swap(early)
         late_swapped = swap(late)
         fold = late[:, 3 * width : 3 * width + channels].reshape(-1, 8, channels)

time: 318 us -> 316 us (level); the launches traced: 317 us -> 309 us
  blocking collectives: 9.65 us -> 0 us
  Pallas kernels: 154 us -> 145 us
  waiting for transfers between devices: 58.7 us -> 66.7 us
    all_to_all x1 -> x0, blocking collectives: 9.65 us -> none  [exchange(): return lax.all_to_all(value, 'res', split_axis=0, concat_axis=0, tiled=True)]
    pallas_call x15 -> x16, Pallas kernels: 154 us -> 145 us  [call(): pl.pallas_call(body, grid_spec=spec, out_shape=[(pltpu.HBM if name in PIN...]
    all_to_all x3 -> x4, waiting for transfers between devices: 8.64 us -> 15.6 us  [exchange(): return lax.all_to_all(value, 'res', split_axis=0, concat_axis=0, tiled=True)]
    ppermute x3, waiting for transfers between devices: 6.31 us -> 10.4 us  [block_parts(): parts.append(lax.ppermute(part, 'res', pairs))]
    psum x1, waiting for transfers between devices: 9.01 us -> 13 us  [per_device(): early = jnp.concatenate(lax.psum((early[:cut], early[cut:]), 'res'), axis=0)]
    ppermute x3, waiting for transfers between devices: 3.42 us -> 0.01 us  [block_gather(): parts.append(lax.ppermute(own, 'res', pairs))]
    all_to_all x3 -> x4, starting transfers between devices: 13.9 us -> 17.3 us  [exchange(): return lax.all_to_all(value, 'res', split_axis=0, concat_axis=0, tiled=True)]
    unnamed x99 -> x108, local copies, waits for them, and re-layouts: 8.03 us -> 8.37 us
  transfers between devices with their start and end apart: 55 -> 54, of which waited for: 20 -> 16; matrix products, arithmetic and copies ran while one was open for 3% -> 3% of each run, Pallas kernels for 45% -> 43%
where the time goes in v1:
time: 316 us; the launch traced here: 309 us
  Pallas kernels  145 us (46%)
  waiting for transfers between devices  66.7 us (21%)
  starting transfers between devices  63.4 us (20%)
  between operations  14.7 us (5%)
  local copies, waits for them, and re-layouts  11.8 us (4%)
  other arithmetic  7.29 us (2%)
    pallas_call x16, Pallas kernels, call(): pl.pallas_call(body, grid_spec=spec, out_shape=[(pltpu.HBM if name in PIN...  145 us
    ppermute x30, starting transfers between devices, across(): return lax.ppermute(value, 'mp', pairs)  35.8 us
    ppermute x30, waiting for transfers between devices, across(): return lax.ppermute(value, 'mp', pairs)  25.3 us
    all_to_all x4, starting transfers between devices, exchange(): return lax.all_to_all(value, 'res', split_axis=0, concat_axis=0, tiled=True)  17.3 us
    all_to_all x4, waiting for transfers between devices, exchange(): return lax.all_to_all(value, 'res', split_axis=0, concat_axis=0, tiled=True)  15.6 us
    psum x1, waiting for transfers between devices, per_device(): early = jnp.concatenate(lax.psum((early[:cut], early[cut:]), 'res'), axis=0)  13 us
    ppermute x3, waiting for transfers between devices, block_parts(): parts.append(lax.ppermute(part, 'res', pairs))  10.4 us
    unnamed x108, local copies, waits for them, and re-layouts  8.37 us
  transfers between devices with their start and end apart: 54, of which 16 were waited for; matrix products, arithmetic and copies ran while one was open for 3% of the time, Pallas kernels for 43%

profile of v1, /device:TPU:0, one launch (start us, length us, event | category | flops | bytes accessed | tf_op | source)
XLA Modules:
  0.0 309.5 jit_solution(7616123052017350789)
XLA Ops:
  7.9 3.5 %pack.1 = (bf16[64,1664]{1,0:T(8,128)(2,1)}, bf16[4,4,16,512]{3,2,1,0:T(8,128)(2,1)}) custom-call(s32[6]{0:T(128)} %stack.57.perm_ref, bf16[2,512,128]{2,1,0:T(8,128)(2,1)} %nodes_ref.1, bf16[128,512]{1,0:T(8,128)(2,1)} %output_ref.2, bf16[128]{0:T(256)(128)(2,1)} %bias_ref.1, s32[4,1,4,16]{3,2,1,0:T(4,128)} %send_ref.3, bf16[4,256,512]{2,1,0:T(8,128)(2,1)} %refs_19_.1), custom_call_target="tpu_custom_call" | custom-call | tf_op jit(solution)/shard_map/pack/pallas_call | solution.py:780
  11.4 2.9 collective-permute-start
  14.3 1.5 collective-permute-start.1
  15.8 5.3 %all-to-all-start = ((bf16[4,4,16,512]{3,2,1,0:T(8,128)(2,1)}), bf16[4,4,16,512]{3,2,1,0:T(8,128)(2,1)S(1)}, u32[]{:S(2)}, u32[]{:S(2)}) async-start(bf16[4,4,16,512]{3,2,1,0:T(8,128)(2,1)} %get-tuple-element.173), calls=%async_computation | async-start | bytes 524288 | tf_op jit(solution)/shard_map/all_to_all | solution.py:805
  21.2 4.2 %prepare.1 = (bf16[192,512]{1,0:T(8,128)(2,1)}, bf16[512,192]{1,0:T(8,128)(2,1)}, f32[192,128]{1,0:T(8,128)}, bf16[192,208]{1,0:T(8,128)(2,1)}, bf16[192,192]{1,...) custom-call(s32[6]{0:T(128)} %stack.57.perm_ref, ...), custom_call_target="tpu_custom_call" | custom-call | tf_op jit(solution)/shard_map/prepare/pallas_call | solution.py:780
  27.0 3.7 %all-to-all-done.refs_3_.refs_18_.refs_20_ = bf16[4,4,16,512]{3,2,1,0:T(8,128)(2,1)S(1)} async-done(((bf16[4,4,16,512]{3,2,1,0:T(8,128)(2,1)}), bf16[4,4,16,512]{3,2,1,0:T(8,128)(2,1)S(1)}, u32[]{:S(2)}, u32[]{:S(2)}) %all-to-all-start) | async-done | bytes 262176 | tf_op jit(solution)/shard_map/all_to_all | solution.py:805
  30.8 1.6 collective-permute-start.10
  32.3 1.5 collective-permute-start.11
  34.4 19.2 %message_forward.2 = (bf16[3,15,512,256]{3,2,1,0:T(8,128)(2,1)}, bf16[3,512,256]{2,1,0:T(8,128)(2,1)}, bf16[256,512]{1,0:T(8,128)(2,1)}, bf16[256,512]{1,0:T(8,128)(2,1)}, bf16[256,512]{1,0:T(8,128)(2,1)}) custom-call(s32[6]{0:T(128)} %stack.57.perm_ref, bf16[4,15,192,256]{3,2,1,0:T(8,128)(2,1)} %bitcast.56, s32[4,15,256]{2,1,0:T(8,128)} %fusion.1.refs_1_, ...), custom_call_target="tpu_custom_call" | custom-call | flops 6039797760 | bytes 16220160 | tf_op jit(solution)/shard_map/message_forward/pallas_call | solution.py:780
  53.6 2.6 collective-permute-done.11.refs_11_.refs_10_
  57.1 1.6 pad_maximum_fusion
  58.8 1.3 collective-permute-start.7
  60.9 1.5 collective-permute-start.9
  62.4 9.0 %message_forward.3 = (bf16[1,15,512,256]{3,2,1,0:T(8,128)(2,1)}, bf16[1,512,256]{2,1,0:T(8,128)(2,1)}, bf16[256,512]{1,0:T(8,128)(2,1)}) custom-call(s32[6]{0:T(128)} %stack.57.perm_ref, bf16[4,15,192,256]{3,2,1,0:T(8,128)(2,1)} %bitcast.57, s32[4,15,256]{2,1,0:T(8,128)} %fusion.1.refs_1_, bf16[4,256,512]{2,1,0:T(8,128)(2,1)} %refs_19_.1, ...), custom_call_target="tpu_custom_call" | custom-call | flops 2013265920 | bytes 5406720 | tf_op jit(solution)/shard_map/message_forward/pallas_call | solution.py:780
  71.4 1.0 collective-permute-done.8.refs_2_
  72.4 1.6 collective-permute-done.9.refs_3_
  74.1 1.3 copy-done.13
  75.4 0.9 copy-done.10
  76.4 5.5 %feed_forward.1 = (f32[256,512]{1,0:T(8,128)S(1)}, f32[256,512]{1,0:T(8,128)S(1)}, bf16[256,512]{1,0:T(8,128)(2,1)}, bf16[256,512]{1,0:T(8,128)(2,1)}, bf16[64,5...) custom-call(bf16[256,512]{1,0:T(8,128)(2,1)S(1)} %copy-done.10, ...), custom_call_target="tpu_custom_call" | custom-call | flops 1073741824 | bytes 4194304 | tf_op jit(solution)/shard_map/feed_forward/pallas_call | solution.py:780
  82.0 3.9 %all-to-all-start.1 = ((bf16[4,16,512]{2,1,0:T(8,128)(2,1)}), bf16[4,16,512]{2,1,0:T(8,128)(2,1)S(1)}, u32[]{:S(2)}, u32[]{:S(2)}) async-start(bf16[4,16,512]{2,1,0:T(8,128)(2,1)} %bitcast.14), calls=%async_computation.1 | async-start | bytes 131072 | tf_op jit(solution)/shard_map/all_to_all | solution.py:805
  86.5 5.0 %all-to-all-done.1 = bf16[4,16,512]{2,1,0:T(8,128)(2,1)S(1)} async-done(((bf16[4,16,512]{2,1,0:T(8,128)(2,1)}), bf16[4,16,512]{2,1,0:T(8,128)(2,1)S(1)}, u32[]{:S(2)}, u32[]{:S(2)}) %all-to-all-start.1) | async-done | bytes 65568 | tf_op jit(solution)/shard_map/all_to_all | solution.py:805
  92.4 1.5 collective-permute-start.15
  93.9 1.2 collective-permute-start.16
  95.2 11.4 %edge_update.2 = (bf16[4,15,192,256]{3,2,1,0:T(8,128)(2,1)}, bf16[1,15,192,256]{3,2,1,0:T(8,128)(2,1)}, bf16[192,576]{1,0:T(8,128)(2,1)}, f32[192,768]{1,0:T(8,128)}) custom-call(s32[6]{0:T(128)} %stack.57.perm_ref, bf16[4,15,192,256]{3,2,1,0:T(8,128)(2,1)} %bitcast.58, s32[4,15,256]{2,1,0:T(8,128)} %fusion.1.refs_1_, bf16[4,15,192,256]{3,2,1,0:T(8,128)(2,1)} %bitcast.63, ...), custom_call_target="tpu_custom_call" | custom-call | flops 2642411520 | bytes 5898240 | tf_op jit(solution)/shard_map/edge_update/pallas_call | solution.py:780
  107.5 29.9 %edge_update.3 = (bf16[4,15,192,256]{3,2,1,0:T(8,128)(2,1)}, bf16[3,15,192,256]{3,2,1,0:T(8,128)(2,1)}, bf16[192,576]{1,0:T(8,128)(2,1)}, bf16[192,576]{1,0:T(8,...) custom-call(s32[6]{0:T(128)} %stack.57.perm_ref, ...), custom_call_target="tpu_custom_call", output_to_operand_aliasing={{0}: (13, {})} | custom-call | flops 7927234560 | bytes 17694720 | tf_op jit(solution)/shard_map/edge_update/pallas_call | solution.py:780
  138.2 1.5 collective-permute-start.18
  139.7 1.2 collective-permute-start.19
  140.9 5.6 %collective-permute-done.17.refs_1_ = bf16[192,576]{1,0:T(8,128)(2,1)S(1)} collective-permute-done((bf16[192,576]{1,0:T(8,128)(2,1)}, bf16[192,576]{1,0:T(8,128)(2,1)S(1)}, u32[]{:S(2)}, u32[]{:S(2)}) %collective-permute-start.17) | collective-permute-done | bytes 221216 | tf_op jit(solution)/shard_map/ppermute | solution.py:796
  146.5 4.7 %collective-permute-done.19.refs_3_ = bf16[192,576]{1,0:T(8,128)(2,1)S(1)} collective-permute-done((bf16[192,576]{1,0:T(8,128)(2,1)}, bf16[192,576]{1,0:T(8,128)(2,1)S(1)}, u32[]{:S(2)}, u32[]{:S(2)}) %collective-permute-start.19) | collective-permute-done | bytes 221216 | tf_op jit(solution)/shard_map/ppermute | solution.py:796
  152.0 3.5 %update_return.1 = (f32[256,512]{1,0:T(8,128)}, bf16[64,512]{1,0:T(8,128)(2,1)}, f32[192,576]{1,0:T(8,128)}) custom-call(s32[6]{0:T(128)} %stack.57.perm_ref, bf16[192,576]{1,0:T(8,128)(2,1)} %get-tuple-element.227.refs_0_, bf16[192,576]{1,0:T(8,128)(2,1)} %copy-done.40, bf16[192,576]{1,0:T(8,128)(2,1)} %copy-done.41, bf16[192,576]{1,0:T(8,128)(2,1)} %copy-done.42, ...), custom_call_target="tpu_custom_call" | custom-call | flops 113246208 | bytes 589824 | tf_op jit(solution)/shard_map/update_return/pallas_call | solution.py:780
  155.4 4.7 %all-to-all-start.2 = ((bf16[4,16,512]{2,1,0:T(8,128)(2,1)}), bf16[4,16,512]{2,1,0:T(8,128)(2,1)S(1)}, u32[]{:S(2)}, u32[]{:S(2)}) async-start(bf16[4,16,512]{2,1,0:T(8,128)(2,1)} %bitcast.78), calls=%async_computation.2 | async-start | bytes 131072 | tf_op jit(solution)/shard_map/all_to_all | solution.py:805
  160.6 3.3 %update_weights.1.refs_26_ = f32[192,1536]{1,0:T(8,128)} custom-call(s32[6]{0:T(128)} %stack.57.perm_ref, f32[192,576]{1,0:T(8,128)} %get-tuple-element.233.sum_ref, bf16[256,512]{1,0:T(8,128)(2,1)} %get-tuple-element.234.low_ref, bf16[64,512]{1,0:T(8,128)(2,1)} %bitcast.71, f32[192,768]{1,0:T(8,128)} %get-tuple-element.235.grad_ref, ...), custom_call_target="tpu_custom_call" | custom-call | flops 113246208 | bytes 589824 | tf_op jit(solution)/shard_map/update_weights/pallas_call | solution.py:780
  163.9 2.0 all-to-all-done.2
  165.9 5.1 %feed_backward.1 = (bf16[256,512]{1,0:T(8,128)(2,1)S(1)}, bf16[272,512]{1,0:T(8,128)(2,1)}, f32[256,512]{1,0:T(8,128)S(1)}, f32[16,512]{1,0:T(8,128)}) custom-call(f32[256,512]{1,0:T(8,128)S(1)} %copy-done.5, bf16[64,512]{1,0:T(8,128)(2,1)S(1)} %bitcast.55, bf16[64,256]{1,0:T(8,128)(2,1)S(1)} %copy-done.8, f32[256,512]{1,0:T(8,128)S(1)} %get-tuple-element.238.refs_3_, ...), custom_call_target="tpu_custom_call" | custom-call | flops 1610612736 | bytes 4194304 | tf_op jit(solution)/shard_map/feed_backward/pallas_call | solution.py:780
  172.9 2.4 collective-permute-start.22
  175.3 9.6 %message_backward.2 = (bf16[4,15,192,256]{3,2,1,0:T(8,128)(2,1)}, bf16[320,512]{1,0:T(8,128)(2,1)}, bf16[1024,320]{1,0:T(8,128)(2,1)}, f32[512,192]{1,0:T(8,128)}) custom-call(s32[6]{0:T(128)} %stack.57.perm_ref, bf16[4,15,192,256]{3,2,1,0:T(8,128)(2,1)} %bitcast.60, s32[4,15,256]{2,1,0:T(8,128)} %fusion.1.refs_1_, ...), custom_call_target="tpu_custom_call" | custom-call | flops 2768240640 | bytes 8355840 | tf_op jit(solution)/shard_map/message_backward/pallas_call | solution.py:780
  185.8 25.2 %message_backward.3 = (bf16[4,15,192,256]{3,2,1,0:T(8,128)(2,1)}, bf16[320,512]{1,0:T(8,128)(2,1)}, bf16[320,512]{1,0:T(8,128)(2,1)}, bf16[320,512]{1,0:T(8,128)...) custom-call(s32[6]{0:T(128)} %stack.57.perm_ref, ...), custom_call_target="tpu_custom_call", output_to_operand_aliasing={{0}: (28, {})} | custom-call | flops 8304721920 | bytes 25067520 | tf_op jit(solution)/shard_map/message_backward/pallas_call | solution.py:780
  212.4 2.3 collective-permute-start.25
  214.7 2.1 fusion.3
  216.9 1.0 slice_bitcast_fusion.1
  217.9 6.7 %feed_weights.1 = (f32[544,512]{1,0:T(8,128)}, bf16[544,512]{1,0:T(8,128)(2,1)}) custom-call(s32[6]{0:T(128)} %stack.57.perm_ref, bf16[1024,512]{1,0:T(8,128)(2,1)} %all-gather.5.cloned.1.call-done.low_ref, bf16[1088,512]{1,0:T(8,128)(2,1)} %all-gather.7.cloned.1.call-done.forward_ref, bf16[512,512]{1,0:T(8,128)(2,1)} %weight_ref.1, ...), custom_call_target="tpu_custom_call" | custom-call | flops 2684354560 | bytes 4194304 | tf_op jit(solution)/shard_map/feed_weights/pallas_call | solution.py:780
  224.5 4.4 %collective-permute-done.24 = bf16[320,512]{1,0:T(8,128)(2,1)S(1)} collective-permute-done((bf16[320,512]{1,0:T(8,128)(2,1)}, bf16[320,512]{1,0:T(8,128)(2,1)S(1)}, u32[]{:S(2)}, u32[]{:S(2)}) %collective-permute-start.24) | collective-permute-done | bytes 327712 | tf_op jit(solution)/shard_map/ppermute | solution.py:796
  228.9 1.3 collective-permute-start.28
  230.7 1.8 collective-permute-start.30
  233.5 3.4 %all-to-all-start.3 = ((bf16[4,16,512]{2,1,0:T(8,128)(2,1)}), bf16[4,16,512]{2,1,0:T(8,128)(2,1)S(1)}, u32[]{:S(2)}, u32[]{:S(2)}) async-start(bf16[4,16,512]{2,1,0:T(8,128)(2,1)} %bitcast.24), calls=%async_computation.3 | async-start | bytes 131072 | tf_op jit(solution)/shard_map/all_to_all | solution.py:805
  237.7 4.9 %all-to-all-done.3 = bf16[4,16,512]{2,1,0:T(8,128)(2,1)S(1)} async-done(((bf16[4,16,512]{2,1,0:T(8,128)(2,1)}), bf16[4,16,512]{2,1,0:T(8,128)(2,1)S(1)}, u32[]{:S(2)}, u32[]{:S(2)}) %all-to-all-start.3) | async-done | bytes 65568 | tf_op jit(solution)/shard_map/all_to_all | solution.py:805
  242.8 5.2 %collective-permute-done.29 = bf16[96,1792]{1,0:T(8,128)(2,1)} collective-permute-done((bf16[96,1792]{1,0:T(8,128)(2,1)}, bf16[96,1792]{1,0:T(8,128)(2,1)}, u32[]{:S(2)}, u32[]{:S(2)}) %collective-permute-start.29) | collective-permute-done | bytes 344096 | tf_op jit(solution)/shard_map/ppermute | solution.py:796
  248.1 1.3 fusion.2
  249.4 1.9 collective-permute-start.33
  252.4 1.1 collective-permute-start.34
  254.2 1.9 collective-permute-done.33
  256.0 1.1 collective-permute-start.36
  257.2 8.5 %collective-permute-done.32 = bf16[24,1792]{1,0:T(8,128)(2,1)S(1)} collective-permute-done((bf16[24,1792]{1,0:T(8,128)(2,1)S(1)}, bf16[24,1792]{1,0:T(8,128)(2,1)S(1)}, u32[]{:S(2)}, u32[]{:S(2)}) %collective-permute-start.32) | collective-permute-done | bytes 86048 | tf_op jit(solution)/shard_map/ppermute | solution.py:816
  265.8 2.6 collective-permute-start.37
  268.4 2.6 collective-permute-start.38
  271.1 3.4 %place_rows.1 = bf16[4,256,512]{2,1,0:T(8,128)(2,1)} custom-call(s32[6]{0:T(128)} %stack.57.perm_ref, bf16[256,512]{1,0:T(8,128)(2,1)} %copy-done.30, bf16[256,512]{1,0:T(8,128)(2,1)} %copy-done.37, bf16[256,512]{1,0:T(8,128)(2,1)} %copy-done.38, bf16[256,512]{1,0:T(8,128)(2,1)} %copy-done.39), custom_call_target="tpu_custom_call" | custom-call | tf_op jit(solution)/shard_map/place_rows/pallas_call | solution.py:780
  274.5 13.0 %all-reduce.3.cloned.1.call-done = (bf16[272,512]{1,0:T(8,128)(2,1)}, bf16[272,512]{1,0:T(8,128)(2,1)}) async-done(((bf16[272,512]{1,0:T(8,128)(2,1)}, bf16[272,512]{1,0:T(8,128)(2,1)}), (bf16[272,512]{1,0:T(8,128)(2,1)}, bf16[272,512]{1,0:T(8,128)(2,1)})) %all-reduce.3.cloned.1.call-update) | async-done | bytes 557072 | tf_op jit(solution)/shard_map/psum | solution.py:1294
  287.5 1.1 pad_maximum_fusion.1.mine_ref
  290.4 1.5 collective-permute-start.42
  291.9 1.3 collective-permute-start.43
  294.0 3.6 %feed_weights_out.1 = (f32[512,512]{1,0:T(8,128)}, f32[512,512]{1,0:T(8,128)}, f32[1,512]{1,0:T(1,128)}, f32[2,512]{1,0:T(2,128)}, f32[2,512]{1,0:T(2,128)}, /*index=5*/f32[2,512]{1,0:T(2,128)}) custom-call(s32[6]{0:T(128)} %stack.57.perm_ref, bf16[544,512]{1,0:T(8,128)(2,1)} %copy-done.19, bf16[544,512]{1,0:T(8,128)(2,1)} %copy-done.32), custom_call_target="tpu_custom_call" | custom-call | bytes 4456448 | tf_op jit(solution)/shard_map/feed_weights_out/pallas_call | solution.py:780
  297.7 1.7 collective-permute-done.45.other_parts_ref
  299.4 2.4 message_weights_out.1
  301.8 1.0 copy.65
  (198 shorter events, 20.3 us)
Async XLA Ops:
  7.2 18.2 %copy-start = (s32[4,256,60]{1,0,2:T(4,128)S(1)}, s32[4,256,60]{1,0,2:T(4,128)}, u32[]{:S(2)}) copy-start(s32[4,256,60]{1,0,2:T(4,128)} %param.25) | copy-start | bytes 737284
  11.4 14.0 %collective-permute-start = (bf16[64,1664]{1,0:T(8,128)(2,1)}, bf16[64,1664]{1,0:T(8,128)(2,1)S(1)}, u32[]{:S(2)}, u32[]{:S(2)}) collective-permute-start(bf16[64,1664]{1,0:T(8,128)(2,1)} %get-tuple-element.190.refs_6_), channel_id=1, source_target_pairs={{0,1},{1,0},{2,3},{3,2},{4,5},{5,4},{6,7},{7,6},{8,9},{9,8},{10,11... | collective-permute-start | bytes 638984 | tf_op jit(solution)/shard_map/ppermute | solution.py:796
  14.3 11.5 %collective-permute-start.1 = (bf16[64,1664]{1,0:T(8,128)(2,1)}, bf16[64,1664]{1,0:T(8,128)(2,1)S(1)}, u32[]{:S(2)}, u32[]{:S(2)}) collective-permute-start(bf16[64,1664]{1,0:T(8,128)(2,1)} %get-tuple-element.190.refs_6_), channel_id=1, source_target_pairs={{0,2},{1,3},{2,0},{3,1},{4,6},{5,7},{6,4},{7,5},{8,10},{9,11},{10,... | collective-permute-start | bytes 638984 | tf_op jit(solution)/shard_map/ppermute | solution.py:796
  15.8 10.2 %collective-permute-start.2 = (bf16[64,1664]{1,0:T(8,128)(2,1)}, bf16[64,1664]{1,0:T(8,128)(2,1)S(1)}, u32[]{:S(2)}, u32[]{:S(2)}) collective-permute-start(bf16[64,1664]{1,0:T(8,128)(2,1)} %get-tuple-element.190.refs_6_), channel_id=1, source_target_pairs={{0,3},{1,2},{2,1},{3,0},{4,7},{5,6},{6,5},{7,4},{8,11},{9,10},{10,... | collective-permute-start | bytes 638984 | tf_op jit(solution)/shard_map/ppermute | solution.py:796
  15.8 11.2 %collective-permute-start.3 = (bf16[64,1664]{1,0:T(8,128)(2,1)}, bf16[64,1664]{1,0:T(8,128)(2,1)S(1)}, u32[]{:S(2)}, u32[]{:S(2)}) collective-permute-start(bf16[64,1664]{1,0:T(8,128)(2,1)} %get-tuple-element.190.refs_6_), channel_id=1, source_target_pairs={{0,16},{16,0},{1,17},{17,1},{2,18},{18,2},{3,19},{19,3},{4,20},{20... | collective-permute-start | bytes 638984 | tf_op jit(solution)/shard_map/ppermute | solution.py:833
  15.8 14.9 %all-to-all-start = ((bf16[4,4,16,512]{3,2,1,0:T(8,128)(2,1)}), bf16[4,4,16,512]{3,2,1,0:T(8,128)(2,1)S(1)}, u32[]{:S(2)}, u32[]{:S(2)}) async-start(bf16[4,4,16,512]{3,2,1,0:T(8,128)(2,1)} %get-tuple-element.173), calls=%async_computation | async-start | bytes 524288 | tf_op jit(solution)/shard_map/all_to_all | solution.py:805
  21.2 116.2 %all-gather.5.cloned.1.call-start = ((), (), s32[]{:S(2)}) async-start(), calls=%async_computation.4 | async-start | bytes 1310720 | tf_op jit(solution)/shard_map/all_gather | solution.py:1068
  25.4 5.3 %collective-permute-start.4 = (bf16[64,1664]{1,0:T(8,128)(2,1)S(1)}, bf16[64,1664]{1,0:T(8,128)(2,1)S(1)}, u32[]{:S(2)}, u32[]{:S(2)}) collective-permute-start(bf16[64,1664]{1,0:T(8,128)(2,1)S(1)} %collective-permute-done.refs_7_), channel_id=1, source_target_pairs={{0,16},{16,0},{1,17},{17,1},{2,18},{18,2},{3,19},{19,3},{4,20},{20... | collective-permute-start | bytes 638984 | tf_op jit(solution)/shard_map/ppermute | solution.py:833
  25.8 4.9 %collective-permute-start.5 = (bf16[64,1664]{1,0:T(8,128)(2,1)S(1)}, bf16[64,1664]{1,0:T(8,128)(2,1)S(1)}, u32[]{:S(2)}, u32[]{:S(2)}) collective-permute-start(bf16[64,1664]{1,0:T(8,128)(2,1)S(1)} %collective-permute-done.1.refs_8_), channel_id=1, source_target_pairs={{0,16},{16,0},{1,17},{17,1},{2,18},{18,2},{3,19},{19,3},{4,20},{20... | collective-permute-start | bytes 638984 | tf_op jit(solution)/shard_map/ppermute | solution.py:833
  26.0 4.8 %collective-permute-start.6 = (bf16[64,1664]{1,0:T(8,128)(2,1)S(1)}, bf16[64,1664]{1,0:T(8,128)(2,1)S(1)}, u32[]{:S(2)}, u32[]{:S(2)}) collective-permute-start(bf16[64,1664]{1,0:T(8,128)(2,1)S(1)} %collective-permute-done.2.refs_9_), channel_id=1, source_target_pairs={{0,16},{16,0},{1,17},{17,1},{2,18},{18,2},{3,19},{19,3},{4,20},{20... | collective-permute-start | bytes 638984 | tf_op jit(solution)/shard_map/ppermute | solution.py:833
  30.8 22.8 %collective-permute-start.10 = (bf16[528,512]{1,0:T(8,128)(2,1)}, bf16[528,512]{1,0:T(8,128)(2,1)S(1)}, u32[]{:S(2)}, u32[]{:S(2)}) collective-permute-start(bf16[528,512]{1,0:T(8,128)(2,1)} %get-tuple-element.209.refs_9_.refs_8_), channel_id=1, source_target_pairs={{0,1},{1,0},{2,3},{3,2},{4,5},{5,4},{6,7},{7,6},{8,9},{9,8},{10,11... | collective-permute-start | bytes 1622024 | tf_op jit(solution)/shard_map/ppermute | solution.py:796
  32.3 23.9 %collective-permute-start.11 = (bf16[528,512]{1,0:T(8,128)(2,1)}, bf16[528,512]{1,0:T(8,128)(2,1)S(1)}, u32[]{:S(2)}, u32[]{:S(2)}) collective-permute-start(bf16[528,512]{1,0:T(8,128)(2,1)} %get-tuple-element.209.refs_9_.refs_8_), channel_id=1, source_target_pairs={{0,2},{1,3},{2,0},{3,1},{4,6},{5,7},{6,4},{7,5},{8,10},{9,11},{10,... | collective-permute-start | bytes 1622024 | tf_op jit(solution)/shard_map/ppermute | solution.py:796
  33.8 22.4 %collective-permute-start.12 = (bf16[528,512]{1,0:T(8,128)(2,1)}, bf16[528,512]{1,0:T(8,128)(2,1)S(1)}, u32[]{:S(2)}, u32[]{:S(2)}) collective-permute-start(bf16[528,512]{1,0:T(8,128)(2,1)} %get-tuple-element.209.refs_9_.refs_8_), channel_id=1, source_target_pairs={{0,3},{1,2},{2,1},{3,0},{4,7},{5,6},{6,5},{7,4},{8,11},{9,10},{10,... | collective-permute-start | bytes 1622024 | tf_op jit(solution)/shard_map/ppermute | solution.py:796
  34.4 22.8 %copy-start.14 = (bf16[528,512]{1,0:T(8,128)(2,1)S(1)}, bf16[528,512]{1,0:T(8,128)(2,1)}, u32[]{:S(2)}) copy-start(bf16[528,512]{1,0:T(8,128)(2,1)} %get-tuple-element.209.refs_9_.refs_8_) | copy-start | bytes 1622020
  58.8 15.3 %collective-permute-start.13 = (bf16[4,528,512]{2,1,0:T(8,128)(2,1)}, bf16[4,528,512]{2,1,0:T(8,128)(2,1)S(1)}, u32[]{:S(2)}, u32[]{:S(2)}) collective-permute-start(bf16[4,528,512]{2,1,0:T(8,128)(2,1)} %pad_maximum_fusion), channel_id=1, source_target_pairs={{0,16},{16,0},{1,17},{17,1},{2,18},{18,2},{3,19},{19,3},{4,20},{20... | collective-permute-start | bytes 6488072 | tf_op jit(solution)/shard_map/ppermute | solution.py:833
  58.8 12.7 %collective-permute-start.7 = (bf16[256,512]{1,0:T(8,128)(2,1)S(1)}, bf16[256,512]{1,0:T(8,128)(2,1)S(1)}, u32[]{:S(2)}, u32[]{:S(2)}) collective-permute-start(bf16[256,512]{1,0:T(8,128)(2,1)S(1)} %copy-done.46), channel_id=1, source_target_pairs={{0,1},{1,0},{2,3},{3,2},{4,5},{5,4},{6,7},{7,6},{8,9},{9,8},{10,11... | collective-permute-start | bytes 786440 | tf_op jit(solution)/shard_map/ppermute | solution.py:796
  60.0 12.4 %collective-permute-start.8 = (bf16[256,512]{1,0:T(8,128)(2,1)S(1)}, bf16[256,512]{1,0:T(8,128)(2,1)S(1)}, u32[]{:S(2)}, u32[]{:S(2)}) collective-permute-start(bf16[256,512]{1,0:T(8,128)(2,1)S(1)} %copy-done.45), channel_id=1, source_target_pairs={{0,2},{1,3},{2,0},{3,1},{4,6},{5,7},{6,4},{7,5},{8,10},{9,11},{10,... | collective-permute-start | bytes 786440 | tf_op jit(solution)/shard_map/ppermute | solution.py:796
  60.9 14.5 %copy-start.2 = (bf16[1216,192]{0,1:T(8,128)(2,1)S(1)}, bf16[1216,192]{0,1:T(8,128)(2,1)}, u32[]{:S(2)}) copy-start(bf16[1216,192]{0,1:T(8,128)(2,1)} %param.38) | copy-start | bytes 1400836
  60.9 14.5 %copy-start.4 = (f32[256,128]{1,0:T(8,128)S(1)}, f32[256,128]{1,0:T(8,128)}, u32[]{:S(2)}) copy-start(f32[256,128]{1,0:T(8,128)} %get-tuple-element.205.refs_5_) | copy-start | bytes 393220
  60.9 14.5 %copy-start.8 = (bf16[64,256]{1,0:T(8,128)(2,1)S(1)}, bf16[64,256]{1,0:T(8,128)(2,1)}, u32[]{:S(2)}) copy-start(bf16[64,256]{1,0:T(8,128)(2,1)} %get-tuple-element.207.refs_7_.refs_2_) | copy-start | bytes 98308
  60.9 14.5 %copy-start.9 = (bf16[1,256,512]{2,1,0:T(8,128)(2,1)S(1)}, bf16[1,256,512]{2,1,0:T(8,128)(2,1)}, u32[]{:S(2)}) copy-start(bf16[1,256,512]{2,1,0:T(8,128)(2,1)} %get-tuple-element.204.refs_4_) | copy-start | bytes 786436
  60.9 14.5 %copy-start.12 = (f32[8,512]{1,0:T(8,128)S(1)}, f32[8,512]{1,0:T(8,128)}, u32[]{:S(2)}) copy-start(f32[8,512]{1,0:T(8,128)} %get-tuple-element.206.refs_6_) | copy-start | bytes 49156
  60.9 13.1 %collective-permute-start.9 = (bf16[256,512]{1,0:T(8,128)(2,1)S(1)}, bf16[256,512]{1,0:T(8,128)(2,1)S(1)}, u32[]{:S(2)}, u32[]{:S(2)}) collective-permute-start(bf16[256,512]{1,0:T(8,128)(2,1)S(1)} %copy-done.44), channel_id=1, source_target_pairs={{0,3},{1,2},{2,1},{3,0},{4,7},{5,6},{6,5},{7,4},{8,11},{9,10},{10,... | collective-permute-start | bytes 786440 | tf_op jit(solution)/shard_map/ppermute | solution.py:796
  82.0 9.6 %all-to-all-start.1 = ((bf16[4,16,512]{2,1,0:T(8,128)(2,1)}), bf16[4,16,512]{2,1,0:T(8,128)(2,1)S(1)}, u32[]{:S(2)}, u32[]{:S(2)}) async-start(bf16[4,16,512]{2,1,0:T(8,128)(2,1)} %bitcast.14), calls=%async_computation.1 | async-start | bytes 131072 | tf_op jit(solution)/shard_map/all_to_all | solution.py:805
  85.8 125.3 %all-gather.9.cloned.1.call-start = ((), (), s32[]{:S(2)}) async-start(), calls=%async_computation.6 | async-start | bytes 1310720 | tf_op jit(solution)/shard_map/all_gather | solution.py:1069
  91.6 15.0 %copy-start.31 = (bf16[4,16,512]{2,1,0:T(8,128)(2,1)}, bf16[4,16,512]{2,1,0:T(8,128)(2,1)S(1)}, u32[]{:S(2)}) copy-start(bf16[4,16,512]{2,1,0:T(8,128)(2,1)S(1)} %all-to-all-done.1) | copy-start | bytes 196612
  91.6 15.0 %collective-permute-start.14 = (bf16[256,512]{1,0:T(8,128)(2,1)S(1)}, bf16[256,512]{1,0:T(8,128)(2,1)S(1)}, u32[]{:S(2)}, u32[]{:S(2)}) collective-permute-start(bf16[256,512]{1,0:T(8,128)(2,1)S(1)} %pad_maximum_fusion.3.refs_3_), channel_id=1, source_target_pairs={{0,1},{1,0},{2,3},{3,2},{4,5},{5,4},{6,7},{7,6},{8,9},{9,8},{10,11... | collective-permute-start | bytes 786440 | tf_op jit(solution)/shard_map/ppermute | solution.py:796
  92.4 14.2 %collective-permute-start.15 = (bf16[256,512]{1,0:T(8,128)(2,1)S(1)}, bf16[256,512]{1,0:T(8,128)(2,1)S(1)}, u32[]{:S(2)}, u32[]{:S(2)}) collective-permute-start(bf16[256,512]{1,0:T(8,128)(2,1)S(1)} %pad_maximum_fusion.3.refs_3_), channel_id=1, source_target_pairs={{0,2},{1,3},{2,0},{3,1},{4,6},{5,7},{6,4},{7,5},{8,10},{9,11},{10,... | collective-permute-start | bytes 786440 | tf_op jit(solution)/shard_map/ppermute | solution.py:796
  93.9 12.7 %collective-permute-start.16 = (bf16[256,512]{1,0:T(8,128)(2,1)S(1)}, bf16[256,512]{1,0:T(8,128)(2,1)S(1)}, u32[]{:S(2)}, u32[]{:S(2)}) collective-permute-start(bf16[256,512]{1,0:T(8,128)(2,1)S(1)} %pad_maximum_fusion.3.refs_3_), channel_id=1, source_target_pairs={{0,3},{1,2},{2,1},{3,0},{4,7},{5,6},{6,5},{7,4},{8,11},{9,10},{10,... | collective-permute-start | bytes 786440 | tf_op jit(solution)/shard_map/ppermute | solution.py:796
  137.4 9.2 %collective-permute-start.17 = (bf16[192,576]{1,0:T(8,128)(2,1)}, bf16[192,576]{1,0:T(8,128)(2,1)S(1)}, u32[]{:S(2)}, u32[]{:S(2)}) collective-permute-start(bf16[192,576]{1,0:T(8,128)(2,1)} %get-tuple-element.228), channel_id=1, source_target_pairs={{0,1},{1,0},{2,3},{3,2},{4,5},{5,4},{6,7},{7,6},{8,9},{9,8},{10,11... | collective-permute-start | bytes 663560 | tf_op jit(solution)/shard_map/ppermute | solution.py:796
  138.2 8.3 %collective-permute-start.18 = (bf16[192,576]{1,0:T(8,128)(2,1)}, bf16[192,576]{1,0:T(8,128)(2,1)S(1)}, u32[]{:S(2)}, u32[]{:S(2)}) collective-permute-start(bf16[192,576]{1,0:T(8,128)(2,1)} %get-tuple-element.229), channel_id=1, source_target_pairs={{0,2},{1,3},{2,0},{3,1},{4,6},{5,7},{6,4},{7,5},{8,10},{9,11},{10,... | collective-permute-start | bytes 663560 | tf_op jit(solution)/shard_map/ppermute | solution.py:796
  139.7 11.5 %collective-permute-start.19 = (bf16[192,576]{1,0:T(8,128)(2,1)}, bf16[192,576]{1,0:T(8,128)(2,1)S(1)}, u32[]{:S(2)}, u32[]{:S(2)}) collective-permute-start(bf16[192,576]{1,0:T(8,128)(2,1)} %get-tuple-element.230), channel_id=1, source_target_pairs={{0,3},{1,2},{2,1},{3,0},{4,7},{5,6},{6,5},{7,4},{8,11},{9,10},{10,... | collective-permute-start | bytes 663560 | tf_op jit(solution)/shard_map/ppermute | solution.py:796
  155.4 10.5 %all-to-all-start.2 = ((bf16[4,16,512]{2,1,0:T(8,128)(2,1)}), bf16[4,16,512]{2,1,0:T(8,128)(2,1)S(1)}, u32[]{:S(2)}, u32[]{:S(2)}) async-start(bf16[4,16,512]{2,1,0:T(8,128)(2,1)} %bitcast.78), calls=%async_computation.2 | async-start | bytes 131072 | tf_op jit(solution)/shard_map/all_to_all | solution.py:805
  160.2 51.0 %all-gather.7.cloned.1.call-start = ((), (), s32[]{:S(2)}) async-start(), calls=%async_computation.5 | async-start | bytes 1392640 | tf_op jit(solution)/shard_map/all_gather | solution.py:1181
  171.8 13.1 %collective-permute-start.20 = (bf16[256,512]{1,0:T(8,128)(2,1)S(1)}, bf16[256,512]{1,0:T(8,128)(2,1)S(1)}, u32[]{:S(2)}, u32[]{:S(2)}) collective-permute-start(bf16[256,512]{1,0:T(8,128)(2,1)S(1)} %get-tuple-element.241.refs_14_.refs_23_), channel_id=1, source_target_pairs={{0,1},{1,0},{2,3},{3,2},{4,5},{5,4},{6,7},{7,6},{8,9},{9,8},{10,11... | collective-permute-start | bytes 786440 | tf_op jit(solution)/shard_map/ppermute | solution.py:796
  172.3 12.6 %collective-permute-start.21 = (bf16[256,512]{1,0:T(8,128)(2,1)S(1)}, bf16[256,512]{1,0:T(8,128)(2,1)S(1)}, u32[]{:S(2)}, u32[]{:S(2)}) collective-permute-start(bf16[256,512]{1,0:T(8,128)(2,1)S(1)} %get-tuple-element.241.refs_14_.refs_23_), channel_id=1, source_target_pairs={{0,2},{1,3},{2,0},{3,1},{4,6},{5,7},{6,4},{7,5},{8,10},{9,11},{10,... | collective-permute-start | bytes 786440 | tf_op jit(solution)/shard_map/ppermute | solution.py:796
  172.9 12.0 %collective-permute-start.22 = (bf16[256,512]{1,0:T(8,128)(2,1)S(1)}, bf16[256,512]{1,0:T(8,128)(2,1)S(1)}, u32[]{:S(2)}, u32[]{:S(2)}) collective-permute-start(bf16[256,512]{1,0:T(8,128)(2,1)S(1)} %get-tuple-element.241.refs_14_.refs_23_), channel_id=1, source_target_pairs={{0,3},{1,2},{2,1},{3,0},{4,7},{5,6},{6,5},{7,4},{8,11},{9,10},{10,... | collective-permute-start | bytes 786440 | tf_op jit(solution)/shard_map/ppermute | solution.py:796
  211.0 3.7 %collective-permute-start.26 = (bf16[4,96,1792]{2,1,0:T(8,128)(2,1)}, bf16[4,96,1792]{2,1,0:T(8,128)(2,1)S(1)}, u32[]{:S(2)}, u32[]{:S(2)}) collective-permute-start(bf16[4,96,1792]{2,1,0:T(8,128)(2,1)} %get-tuple-element.265), channel_id=1, source_target_pairs={{0,16},{16,0},{1,17},{17,1},{2,18},{18,2},{3,19},{19,3},{4,20},{20... | collective-permute-start | bytes 4128776 | tf_op jit(solution)/shard_map/ppermute | solution.py:833
  211.1 13.4 %collective-permute-start.23 = (bf16[320,512]{1,0:T(8,128)(2,1)}, bf16[320,512]{1,0:T(8,128)(2,1)S(1)}, u32[]{:S(2)}, u32[]{:S(2)}) collective-permute-start(bf16[320,512]{1,0:T(8,128)(2,1)} %get-tuple-element.259), channel_id=1, source_target_pairs={{0,1},{1,0},{2,3},{3,2},{4,5},{5,4},{6,7},{7,6},{8,9},{9,8},{10,11... | collective-permute-start | bytes 983048 | tf_op jit(solution)/shard_map/ppermute | solution.py:796
  212.0 16.9 %collective-permute-start.24 = (bf16[320,512]{1,0:T(8,128)(2,1)}, bf16[320,512]{1,0:T(8,128)(2,1)S(1)}, u32[]{:S(2)}, u32[]{:S(2)}) collective-permute-start(bf16[320,512]{1,0:T(8,128)(2,1)} %get-tuple-element.260), channel_id=1, source_target_pairs={{0,2},{1,3},{2,0},{3,1},{4,6},{5,7},{6,4},{7,5},{8,10},{9,11},{10,... | collective-permute-start | bytes 983048 | tf_op jit(solution)/shard_map/ppermute | solution.py:796
  212.4 16.5 %collective-permute-start.25 = (bf16[320,512]{1,0:T(8,128)(2,1)}, bf16[320,512]{1,0:T(8,128)(2,1)S(1)}, u32[]{:S(2)}, u32[]{:S(2)}) collective-permute-start(bf16[320,512]{1,0:T(8,128)(2,1)} %get-tuple-element.261), channel_id=1, source_target_pairs={{0,3},{1,2},{2,1},{3,0},{4,7},{5,6},{6,5},{7,4},{8,11},{9,10},{10,... | collective-permute-start | bytes 983048 | tf_op jit(solution)/shard_map/ppermute | solution.py:796
  217.9 14.6 %copy-start.33 = (bf16[320,512]{1,0:T(8,128)(2,1)S(1)}, bf16[320,512]{1,0:T(8,128)(2,1)}, u32[]{:S(2)}) copy-start(bf16[320,512]{1,0:T(8,128)(2,1)} %get-tuple-element.271) | copy-start | bytes 983044
  228.9 4.4 %collective-permute-start.27 = (bf16[544,512]{1,0:T(8,128)(2,1)}, bf16[544,512]{1,0:T(8,128)(2,1)S(1)}, u32[]{:S(2)}, u32[]{:S(2)}) collective-permute-start(bf16[544,512]{1,0:T(8,128)(2,1)} %get-tuple-element.275), channel_id=1, source_target_pairs={{0,16},{16,0},{1,17},{17,1},{2,18},{18,2},{3,19},{19,3},{4,20},{20... | collective-permute-start | bytes 1671176 | tf_op jit(solution)/shard_map/ppermute | solution.py:833
  228.9 13.9 %collective-permute-start.28 = (bf16[96,1792]{1,0:T(8,128)(2,1)}, bf16[96,1792]{1,0:T(8,128)(2,1)}, u32[]{:S(2)}, u32[]{:S(2)}) collective-permute-start(bf16[96,1792]{1,0:T(8,128)(2,1)} %get-tuple-element.282), channel_id=1, source_target_pairs={{0,1},{1,0},{2,3},{3,2},{4,5},{5,4},{6,7},{7,6},{8,9},{9,8},{10,11... | collective-permute-start | bytes 1032200 | tf_op jit(solution)/shard_map/ppermute | solution.py:796
  230.3 17.8 %collective-permute-start.29 = (bf16[96,1792]{1,0:T(8,128)(2,1)}, bf16[96,1792]{1,0:T(8,128)(2,1)}, u32[]{:S(2)}, u32[]{:S(2)}) collective-permute-start(bf16[96,1792]{1,0:T(8,128)(2,1)} %get-tuple-element.283), channel_id=1, source_target_pairs={{0,2},{1,3},{2,0},{3,1},{4,6},{5,7},{6,4},{7,5},{8,10},{9,11},{10,... | collective-permute-start | bytes 1032200 | tf_op jit(solution)/shard_map/ppermute | solution.py:796
  230.7 17.4 %collective-permute-start.30 = (bf16[96,1792]{1,0:T(8,128)(2,1)}, bf16[96,1792]{1,0:T(8,128)(2,1)}, u32[]{:S(2)}, u32[]{:S(2)}) collective-permute-start(bf16[96,1792]{1,0:T(8,128)(2,1)} %get-tuple-element.284), channel_id=1, source_target_pairs={{0,3},{1,2},{2,1},{3,0},{4,7},{5,6},{6,5},{7,4},{8,11},{9,10},{10,... | collective-permute-start | bytes 1032200 | tf_op jit(solution)/shard_map/ppermute | solution.py:796
  233.5 9.1 %all-to-all-start.3 = ((bf16[4,16,512]{2,1,0:T(8,128)(2,1)}), bf16[4,16,512]{2,1,0:T(8,128)(2,1)S(1)}, u32[]{:S(2)}, u32[]{:S(2)}) async-start(bf16[4,16,512]{2,1,0:T(8,128)(2,1)} %bitcast.24), calls=%async_computation.3 | async-start | bytes 131072 | tf_op jit(solution)/shard_map/all_to_all | solution.py:805
  236.8 50.7 %all-reduce.3.cloned.1.call-start = ((), (), s32[]{:S(2)}) async-start(), calls=%async_computation.7 | async-start | bytes 1114112 | tf_op jit(solution)/shard_map/psum | solution.py:1294
  242.8 28.2 %copy-start.30 = (bf16[256,512]{1,0:T(8,128)(2,1)}, bf16[256,512]{1,0:T(8,128)(2,1)S(1)}, u32[]{:S(2)}) copy-start(bf16[256,512]{1,0:T(8,128)(2,1)S(1)} %fusion.refs_0_) | copy-start | bytes 786436
  249.4 6.6 %collective-permute-start.33 = (bf16[24,1792]{1,0:T(8,128)(2,1)S(1)}, bf16[24,1792]{1,0:T(8,128)(2,1)S(1)}, u32[]{:S(2)}, u32[]{:S(2)}) collective-permute-start(bf16[24,1792]{1,0:T(8,128)(2,1)S(1)} %get-tuple-element.336), channel_id=1, source_target_pairs={{0,12},{4,0},{8,4},{12,8},{1,13},{5,1},{9,5},{13,9},{2,14},{6,2},{... | collective-permute-start | bytes 258056 | tf_op jit(solution)/shard_map/ppermute | solution.py:816
  251.3 14.4 %collective-permute-start.32 = (bf16[24,1792]{1,0:T(8,128)(2,1)S(1)}, bf16[24,1792]{1,0:T(8,128)(2,1)S(1)}, u32[]{:S(2)}, u32[]{:S(2)}) collective-permute-start(bf16[24,1792]{1,0:T(8,128)(2,1)S(1)} %get-tuple-element.337), channel_id=1, source_target_pairs={{0,8},{4,12},{8,0},{12,4},{1,9},{5,13},{9,1},{13,5},{2,10},{6,14},... | collective-permute-start | bytes 258056 | tf_op jit(solution)/shard_map/ppermute | solution.py:816
  251.8 13.8 %collective-permute-start.31 = (bf16[24,1792]{1,0:T(8,128)(2,1)S(1)}, bf16[24,1792]{1,0:T(8,128)(2,1)S(1)}, u32[]{:S(2)}, u32[]{:S(2)}) collective-permute-start(bf16[24,1792]{1,0:T(8,128)(2,1)S(1)} %get-tuple-element.335), channel_id=1, source_target_pairs={{0,4},{4,8},{8,12},{12,0},{1,5},{5,9},{9,13},{13,1},{2,6},{6,10},{... | collective-permute-start | bytes 258056 | tf_op jit(solution)/shard_map/ppermute | solution.py:816
  252.4 13.3 %collective-permute-start.34 = (bf16[256,512]{1,0:T(8,128)(2,1)S(1)}, bf16[256,512]{1,0:T(8,128)(2,1)S(1)}, u32[]{:S(2)}, u32[]{:S(2)}) collective-permute-start(bf16[256,512]{1,0:T(8,128)(2,1)S(1)} %fusion.refs_0_), channel_id=1, source_target_pairs={{0,1},{1,0},{2,3},{3,2},{4,5},{5,4},{6,7},{7,6},{8,9},{9,8},{10,11... | collective-permute-start | bytes 786440 | tf_op jit(solution)/shard_map/ppermute | solution.py:796
  253.5 12.3 %collective-permute-start.35 = (bf16[256,512]{1,0:T(8,128)(2,1)S(1)}, bf16[256,512]{1,0:T(8,128)(2,1)S(1)}, u32[]{:S(2)}, u32[]{:S(2)}) collective-permute-start(bf16[256,512]{1,0:T(8,128)(2,1)S(1)} %fusion.refs_0_), channel_id=1, source_target_pairs={{0,2},{1,3},{2,0},{3,1},{4,6},{5,7},{6,4},{7,5},{8,10},{9,11},{10,... | collective-permute-start | bytes 786440 | tf_op jit(solution)/shard_map/ppermute | solution.py:796
  256.0 9.8 %collective-permute-start.36 = (bf16[256,512]{1,0:T(8,128)(2,1)S(1)}, bf16[256,512]{1,0:T(8,128)(2,1)S(1)}, u32[]{:S(2)}, u32[]{:S(2)}) collective-permute-start(bf16[256,512]{1,0:T(8,128)(2,1)S(1)} %fusion.refs_0_), channel_id=1, source_target_pairs={{0,3},{1,2},{2,1},{3,0},{4,7},{5,6},{6,5},{7,4},{8,11},{9,10},{10,... | collective-permute-start | bytes 786440 | tf_op jit(solution)/shard_map/ppermute | solution.py:796
  265.8 22.8 %collective-permute-start.37 = (bf16[24,1792]{1,0:T(8,128)(2,1)S(1)}, bf16[24,1792]{1,0:T(8,128)(2,1)S(1)}, u32[]{:S(2)}, u32[]{:S(2)}) collective-permute-start(bf16[24,1792]{1,0:T(8,128)(2,1)S(1)} %add_convert_fusion.1), channel_id=1, source_target_pairs={{0,12},{4,0},{8,4},{12,8},{1,13},{5,1},{9,5},{13,9},{2,14},{6,2},{... | collective-permute-start | bytes 258056 | tf_op jit(solution)/shard_map/ppermute | solution.py:823
  268.4 20.2 %collective-permute-start.38 = (bf16[24,1792]{1,0:T(8,128)(2,1)S(1)}, bf16[24,1792]{1,0:T(8,128)(2,1)S(1)}, u32[]{:S(2)}, u32[]{:S(2)}) collective-permute-start(bf16[24,1792]{1,0:T(8,128)(2,1)S(1)} %add_convert_fusion.1), channel_id=1, source_target_pairs={{0,8},{4,12},{8,0},{12,4},{1,9},{5,13},{9,1},{13,5},{2,10},{6,14},... | collective-permute-start | bytes 258056 | tf_op jit(solution)/shard_map/ppermute | solution.py:823
  271.0 17.6 %collective-permute-start.39 = (bf16[24,1792]{1,0:T(8,128)(2,1)S(1)}, bf16[24,1792]{1,0:T(8,128)(2,1)S(1)}, u32[]{:S(2)}, u32[]{:S(2)}) collective-permute-start(bf16[24,1792]{1,0:T(8,128)(2,1)S(1)} %add_convert_fusion.1), channel_id=1, source_target_pairs={{0,4},{4,8},{8,12},{12,0},{1,5},{5,9},{9,13},{13,1},{2,6},{6,10},{... | collective-permute-start | bytes 258056 | tf_op jit(solution)/shard_map/ppermute | solution.py:823
  288.8 4.3 %collective-permute-start.40 = (bf16[544,512]{1,0:T(8,128)(2,1)S(1)}, bf16[544,512]{1,0:T(8,128)(2,1)S(1)}, u32[]{:S(2)}, u32[]{:S(2)}) collective-permute-start(bf16[544,512]{1,0:T(8,128)(2,1)S(1)} %pad_maximum_fusion.1.mine_ref), channel_id=1, source_target_pairs={{0,16},{16,0},{1,17},{17,1},{2,18},{18,2},{3,19},{19,3},{4,20},{20... | collective-permute-start | bytes 1671176 | tf_op jit(solution)/shard_map/ppermute | solution.py:833
  289.0 8.5 %collective-permute-start.44 = (bf16[64,1792]{1,0:T(8,128)(2,1)S(1)}, bf16[64,1792]{1,0:T(8,128)(2,1)S(1)}, u32[]{:S(2)}, u32[]{:S(2)}) collective-permute-start(bf16[64,1792]{1,0:T(8,128)(2,1)S(1)} %constant_dynamic-slice_fusion.1.mine_ref), channel_id=1, source_target_pairs={{0,16},{16,0},{1,17},{17,1},{2,18},{18,2},{3,19},{19,3},{4,20},{20... | collective-permute-start | bytes 688136 | tf_op jit(solution)/shard_map/ppermute | solution.py:833
  289.6 7.9 %collective-permute-start.41 = (bf16[32,1536]{1,0:T(8,128)(2,1)S(1)}, bf16[32,1536]{1,0:T(8,128)(2,1)S(1)}, u32[]{:S(2)}, u32[]{:S(2)}) collective-permute-start(bf16[32,1536]{1,0:T(8,128)(2,1)S(1)} %pad_maximum_fusion.4), channel_id=1, source_target_pairs={{0,1},{1,0},{2,3},{3,2},{4,5},{5,4},{6,7},{7,6},{8,9},{9,8},{10,11... | collective-permute-start | bytes 294920 | tf_op jit(solution)/shard_map/ppermute | solution.py:796
  290.4 7.1 %collective-permute-start.42 = (bf16[32,1536]{1,0:T(8,128)(2,1)S(1)}, bf16[32,1536]{1,0:T(8,128)(2,1)S(1)}, u32[]{:S(2)}, u32[]{:S(2)}) collective-permute-start(bf16[32,1536]{1,0:T(8,128)(2,1)S(1)} %pad_maximum_fusion.4), channel_id=1, source_target_pairs={{0,2},{1,3},{2,0},{3,1},{4,6},{5,7},{6,4},{7,5},{8,10},{9,11},{10,... | collective-permute-start | bytes 294920 | tf_op jit(solution)/shard_map/ppermute | solution.py:796
  291.9 5.7 %collective-permute-start.43 = (bf16[32,1536]{1,0:T(8,128)(2,1)S(1)}, bf16[32,1536]{1,0:T(8,128)(2,1)S(1)}, u32[]{:S(2)}, u32[]{:S(2)}) collective-permute-start(bf16[32,1536]{1,0:T(8,128)(2,1)S(1)} %pad_maximum_fusion.4), channel_id=1, source_target_pairs={{0,3},{1,2},{2,1},{3,0},{4,7},{5,6},{6,5},{7,4},{8,11},{9,10},{10,... | collective-permute-start | bytes 294920 | tf_op jit(solution)/shard_map/ppermute | solution.py:796
  297.6 1.8 collective-permute-start.45
  (40 other events, 173.2 us)
Sparse Core Ops, SparseCore 0:
  82.1 30.3 all-gather.4
  114.3 26.3 all-gather.8
  175.4 24.7 all-gather.6
  240.9 46.5 all-reduce.2
